TPU v7x, 512 devices: a whole 4x4x16 slice. The times are simulated.
512 devices in a mesh: pb: 32 (over z, core), ka: 16 (over y, x).
Axes of the slice: x: 4, y: 4, z: 16, core: 2. Of those that a mesh axis runs over, the one named last changes fastest.
Arguments:
- teacher_query: bfloat16 [16384, 256], P('pb'), may hold values from -96 to 96
- teacher_key: bfloat16 [16384, 256], P('ka'), may hold values from -8 to 8
- student_c: bfloat16 [16384, 128], P('pb'), may hold values from -0.009 to 0.009
- student_b: bfloat16 [16384, 128], P('ka'), may hold values from -0.009 to 0.009
- decay_rate: float32 [2, 16384], P(None, 'pb'), may hold values from 0 to 1
Outputs:
- grad_c: float32 [16384, 128], P(('pb', 'ka'))
- grad_b: float32 [16384, 128], P(('ka', 'pb'))
- grad_rate: float32 [2, 16384], P(None, 'pb')
All inputs are finite; a program needn't handle non-finite values.
Results may differ from a plain program's by a relative error of at most 0.003.
Values may be sent and summed in bfloat16 or wider, within the bound.
A program may use at most 128 MiB of HBM per device.

v0:
```python
import math

import jax
import jax.numpy as jnp
from jax import lax
from jax.sharding import PartitionSpec as P

NEGATIVE = -1e30


def combined_all(value, axis, combine):
    everything = jax.tree.map(lambda part: lax.all_gather(part, axis), value)
    first = jax.tree.map(lambda part: part[0], everything)

    def combined_turn(k, so_far):
        return combine(so_far, jax.tree.map(lambda part: part[k], everything))

    return lax.fori_loop(1, lax.axis_size(axis), combined_turn, first)


def prefix(value, axis, combine, identity):
    peers, position = (lax.axis_size(axis), lax.axis_index(axis))
    everything = lax.all_gather(value, axis)
    start = jnp.broadcast_to(jnp.asarray(identity, value.dtype), value.shape)

    def prefix_turn(k, before):
        reached = k < position
        new = combine(before, everything[k])
        return jnp.where(reached, new, before)

    return lax.fori_loop(0, peers, prefix_turn, start)


def add_terms(earlier, later):
    return earlier + later


def merge_stats(first, second):
    peak = jnp.maximum(first[0], second[0])
    return (peak, first[1] * jnp.exp(first[0] - peak) + second[1] * jnp.exp(second[0] - peak))


def reverse_sums(values):
    return jnp.cumsum(values[:, ::-1], axis=1)[:, ::-1]


def tile_grads(
    queries, key_rows, c_rows, b_rows, query_pos, key_pos, cum_full, heads, factor, row_limit
):
    query_count = queries.shape[0]
    key_count = key_rows.shape[0]
    query_heads = queries.reshape(query_count, heads, -1)
    key_heads = key_rows.reshape(key_count, heads, -1)
    c_heads = c_rows.reshape(query_count, heads, -1)
    b_heads = b_rows.reshape(key_count, heads, -1)
    state = c_heads.shape[2]
    scale = 1.0 / math.sqrt(query_heads.shape[2])
    cum_query = cum_full[:, query_pos]
    cum_key = cum_full[:, key_pos]
    row_size = min(query_count, row_limit)
    col_size = min(key_count, 256)
    col_steps = key_count // col_size

    def block_mask(col_index):
        cols_here = key_pos[col_index * col_size : (col_index + 1) * col_size]
        return (query_pos[:, None] >= cols_here[None, :])[None]

    def block_scores(col_index):
        right = key_heads[col_index * col_size : (col_index + 1) * col_size]
        return (
            jnp.einsum("qhd,khd->hqk", query_heads, right, preferred_element_type=jnp.float32)
            * scale
        )

    def is_live(row_index, col_index):
        return query_pos[(row_index + 1) * row_size - 1] >= key_pos[col_index * col_size]

    row_index = 0
    peak = jnp.full((heads, row_size), NEGATIVE, jnp.float32)
    running = jnp.zeros((heads, row_size), jnp.float32)
    for col_index in range(col_steps):

        def live_stats(unused, row_index=row_index, col_index=col_index):
            scores = block_scores(col_index)
            mask = block_mask(col_index)
            masked = jnp.where(mask, scores, NEGATIVE)
            block_peak = jnp.max(masked, axis=2)
            block_total = jnp.sum(
                jnp.where(mask, jnp.exp(masked - block_peak[:, :, None]), 0.0), axis=2
            )
            return (block_peak, block_total)

        def empty_stats(unused):
            return (
                jnp.full((heads, row_size), NEGATIVE, jnp.float32),
                jnp.zeros((heads, row_size), jnp.float32),
            )

        block_peak, block_total = lax.cond(
            is_live(row_index, col_index), live_stats, empty_stats, 0
        )
        new_peak = jnp.maximum(peak, block_peak)
        running = running * jnp.exp(peak - new_peak) + block_total * jnp.exp(block_peak - new_peak)
        peak = new_peak
    peak_all = peak
    total_all = running
    peak_all, total_all = combined_all((peak_all, total_all), "ka", merge_stats)
    b_grad_blocks = [
        jnp.zeros((col_size, heads, state), jnp.float32) for col_index in range(col_steps)
    ]
    col_blocks = [jnp.zeros((heads, col_size), jnp.float32) for col_index in range(col_steps)]
    row_index = 0
    c_grad = jnp.zeros((row_size, heads, state), jnp.float32)
    row_total = jnp.zeros((heads, row_size), jnp.float32)
    first_row = row_index * row_size
    last_row = first_row + row_size
    for col_index in range(col_steps):
        first_col = col_index * col_size
        last_col = first_col + col_size

        def live_grads(
            unused,
            row_index=row_index,
            col_index=col_index,
            first_row=first_row,
            last_row=last_row,
            first_col=first_col,
            last_col=last_col,
        ):
            mask = block_mask(col_index)
            scores = block_scores(col_index)
            prob = (
                jnp.exp(jnp.where(mask, scores - peak_all[:, :, None], NEGATIVE))
                / total_all[:, :, None]
            )
            decay = jnp.exp(
                jnp.where(
                    mask,
                    cum_query[:, first_row:last_row, None] - cum_key[:, None, first_col:last_col],
                    NEGATIVE,
                )
            )
            b_here = b_heads[first_col:last_col]
            inner = jnp.einsum("qhn,khn->hqk", c_heads, b_here, preferred_element_type=jnp.float32)
            student = inner * decay
            grad = factor * (student - prob)
            weight = (grad * decay).astype(jnp.bfloat16)
            c_part = jnp.einsum("hqk,khn->qhn", weight, b_here, preferred_element_type=jnp.float32)
            b_part = jnp.einsum("hqk,qhn->khn", weight, c_heads, preferred_element_type=jnp.float32)
            related = grad * student
            return (c_part, b_part, jnp.sum(related, axis=2), jnp.sum(related, axis=1))

        def empty_grads(unused):
            return (
                jnp.zeros((row_size, heads, state), jnp.float32),
                jnp.zeros((col_size, heads, state), jnp.float32),
                jnp.zeros((heads, row_size), jnp.float32),
                jnp.zeros((heads, col_size), jnp.float32),
            )

        c_part, b_part, row_part, col_part = lax.cond(
            is_live(row_index, col_index), live_grads, empty_grads, 0
        )
        c_grad = c_grad + c_part
        row_total = row_total + row_part
        b_grad_blocks[col_index] = b_part
        col_blocks[col_index] = col_blocks[col_index] + col_part
    c_grad_all = c_grad.reshape(query_count, heads * state)
    b_grad_all = jnp.concatenate(b_grad_blocks, axis=0).reshape(key_count, heads * state)
    return (c_grad_all, b_grad_all, row_total, jnp.concatenate(col_blocks, axis=1))


def body(teacher_query, teacher_key, student_c, student_b, decay_rate):
    heads = decay_rate.shape[0]
    query_count = teacher_query.shape[0]
    key_count = teacher_key.shape[0]
    pb_count = lax.axis_size("pb")
    pb_index = lax.axis_index("pb")
    ka_index = lax.axis_index("ka")
    total = query_count * pb_count
    partial_sums = jnp.cumsum(decay_rate, axis=1)
    offset = prefix(partial_sums[:, -1:], "pb", add_terms, jnp.zeros((heads, 1), jnp.float32))
    cum_full = lax.all_gather(-(offset + partial_sums), "pb", axis=1, tiled=True)
    queries, c_rows, key_rows, b_rows = (teacher_query, student_c, teacher_key, student_b)
    query_pos = pb_index * query_count + jnp.arange(query_count, dtype=jnp.int32)
    key_pos = ka_index * key_count + jnp.arange(key_count, dtype=jnp.int32)
    row_limit = 512
    c_grad_all, b_grad_all, row_part, col_part = tile_grads(
        queries,
        key_rows,
        c_rows,
        b_rows,
        query_pos,
        key_pos,
        cum_full,
        heads,
        2.0 * total,
        row_limit,
    )
    grad_c = lax.psum_scatter(c_grad_all, "ka", scatter_dimension=0, tiled=True)
    grad_b = lax.psum_scatter(b_grad_all, "pb", scatter_dimension=0, tiled=True)
    own_query = pb_index * query_count + jnp.arange(query_count, dtype=jnp.int32)
    own_key = ka_index * key_count + jnp.arange(key_count, dtype=jnp.int32)
    slope = (
        jnp.zeros((heads, total), jnp.float32)
        .at[:, own_query]
        .add(row_part)
        .at[:, own_key]
        .add(-col_part)
    )
    slope = lax.psum(slope, ("pb", "ka"))
    tail = reverse_sums(slope)
    grad_rate = -lax.dynamic_slice_in_dim(tail, pb_index * query_count, query_count, 1)
    return (grad_c, grad_b, grad_rate)


def solution(mesh):
    placed = (P("pb", None), P("ka", None), P("pb", None), P("ka", None), P(None, "pb"))
    return jax.shard_map(
        body,
        mesh=mesh,
        in_specs=placed,
        out_specs=(P(("pb", "ka"), None), P(("ka", "pb"), None), P(None, "pb")),
        check_vma=False,
    )
```

profile of v0, /device:TPU:1, one launch (start us, length us, event | category | flops | bytes accessed | tf_op | source)
XLA Modules:
  0.0 742.6 jit_solution(9437635251333083461)
XLA Ops:
  8.7 0.6 fusion.55
  14.4 0.7 reshape.326
  15.1 0.6 reduce-window.14
  16.4 1.3 dynamic-slice
  18.5 53.3 %all-reduce = f32[64]{0:T(128)S(1)} all-reduce(f32[64]{0:T(128)S(1)} %dynamic-update-slice), channel_id=2, replica_groups=mesh['pb'=32,'ka'=16] {'pb'}, use_global_device_ids=true, to_apply=%add | all-reduce | flops 64 | bytes 512
  71.9 1.2 while.32
  73.2 29.9 %all_gather.23 = f32[2,16384]{1,0:T(2,128)S(1)} all-gather(f32[2,512]{1,0:T(2,128)S(1)} %add_negate_fusion), channel_id=1, replica_groups=mesh['pb'=32,'ka'=16] {'pb'}, dimensions={1}, use_global_device_ids=true | all-gather | bytes 135168 | tf_op jit(solution)/shard_map/all_gather | solution.py:183
  103.1 1.0 copy.138
  104.1 1.1 copy.143
  105.2 1.1 copy.137
  106.3 1.2 copy.142
  107.6 2.3 conditional.11
  108.0 0.9 fusion.54
  109.0 0.9 select_reduce_fusion.3
  109.9 2.3 conditional.10
  110.4 0.9 fusion.53
  111.3 0.9 select_reduce_fusion.2
  112.2 2.3 conditional.9
  112.7 0.9 fusion.52
  113.6 0.9 select_reduce_fusion.1
  114.6 2.3 conditional.8
  115.0 0.9 fusion.51
  116.0 0.9 select_reduce_fusion
  116.9 0.8 add_bitcast_fusion.1
  117.7 15.2 %all-gather.4 = f32[16,2,512]{2,1,0:T(2,128)S(1)} all-gather(f32[1,2,512]{2,1,0:T(2,128)S(1)} %get-tuple-element.785), channel_id=4, replica_groups=mesh['pb'=32,'ka'=16] {'ka'}, dimensions={0}, use_global_device_ids=true | all-gather | bytes 69632 | tf_op jit(solution)/shard_map/all_gather | solution.py:12
  132.9 18.3 %all-gather.3 = f32[16,2,512]{2,1,0:T(2,128)S(1)} all-gather(f32[1,2,512]{2,1,0:T(2,128)S(1)} %get-tuple-element.786), channel_id=3, replica_groups=mesh['pb'=32,'ka'=16] {'ka'}, dimensions={0}, use_global_device_ids=true | all-gather | bytes 69632 | tf_op jit(solution)/shard_map/all_gather | solution.py:12
  151.2 0.7 while.31
  151.9 5.0 copy.140
  156.9 4.4 gather_fusion
  161.3 6.2 gather_fusion.1
  167.5 2.9 conditional.15
  168.7 0.8 multiply_reduce_fusion.6
  170.4 2.9 conditional.14
  171.6 0.8 multiply_reduce_fusion.4
  173.3 3.1 conditional.13
  174.7 0.8 multiply_reduce_fusion.2
  176.4 2.9 conditional.12
  177.7 0.8 multiply_reduce_fusion
  179.8 6.0 scatter_custom_fusion
  185.7 12.0 %scatter_fusion = f32[2,16384]{0,1:T(8,128)} fusion(f32[2,16384]{0,1:T(8,128)} %scatter_custom_fusion, s32[1024]{0:T(1024)S(1)} %bitcast.133, f32[1024,2]{1,0:T(8,128)S(1)} %copy.169), kind=kCustom, calls=%fused_computation.3 | custom fusion | flops 2048 | bytes 28672 | tf_op jit(solution)/shard_map/scatter-add | solution.py:209
  197.7 63.4 %rev.6 = f32[2,16384]{0,1:T(8,128)} reverse(f32[2,16384]{0,1:T(8,128)} %scatter_fusion), dimensions={1} | reverse | bytes 262144 | tf_op jit(solution)/shard_map/rev | solution.py:44
  261.2 7.2 copy.170
  268.5 0.8 copy.182
  269.5 1.0 copy.184
  270.5 451.3 %all-reduce.3.cloned.1.call-done = f32[2,128,128]{1,2,0:T(8,128)} async-done(((f32[2,128,128]{1,2,0:T(8,128)}), f32[2,128,128]{1,2,0:T(8,128)}) %all-reduce.3.cloned.1.call-update) | async-done | bytes 131088 | tf_op jit(solution)/shard_map/psum | solution.py:211
  721.8 1.1 reduce-window.16
  723.4 11.1 %rev.7 = f32[2,16384]{1,0:T(2,128)S(1)} reverse(f32[2,16384]{1,0:T(2,128)S(1)} %bitcast.123), dimensions={1} | reverse | bytes 262144 | tf_op jit(solution)/shard_map/rev | solution.py:44
  734.6 0.6 dynamic-slice_negate_fusion
  (134 shorter events, 13.9 us)
Async XLA Ops:
  8.0 713.8 %all-reduce.3.cloned.1.call-start = ((), (), s32[]{:S(2)}) async-start(), calls=%async_computation.2 | async-start | bytes 262144 | tf_op jit(solution)/shard_map/psum | solution.py:211
  268.4 466.8 %reduce-scatter.7.cloned.1.call-start = ((), (), s32[]{:S(2)}) async-start(), calls=%async_computation.3 | async-start | bytes 278528
  269.4 465.8 %reduce-scatter.9.cloned.1.call-start = ((), (), s32[]{:S(2)}) async-start(), calls=%async_computation.4 | async-start | bytes 540672
Sparse Core Ops, SparseCore 0:
  268.5 453.2 all-reduce.2
Sparse Core Ops, SparseCore 1:
  273.4 89.4 reduce-scatter.6
  366.4 106.4 reduce-scatter.8
where the time goes:
time: 748 us; the launch traced here: 743 us
  waiting for transfers between devices  451 us (60%)
  blocking collectives  117 us (16%)
  local copies, waits for them, and re-layouts  111 us (15%)
  other arithmetic  27.6 us (4%)
  between operations  21.5 us (3%)
  matrix products  12.3 us (2%)
    psum x1, waiting for transfers between devices, body(): slope = lax.psum(slope, ('pb', 'ka'))  451 us
    rev x2, local copies, waits for them, and re-layouts, reverse_sums(): return jnp.cumsum(values[:, ::-1], axis=1)[:, ::-1]  74.6 us
    unnamed x1, blocking collectives  53.3 us
    all_gather x2, blocking collectives, combined_all(): everything = jax.tree.map(lambda part: lax.all_gather(part, axis), value)  33.5 us
    all_gather x1, blocking collectives, body(): lax.all_gather(-(offset + partial_sums), 'pb', axis=1, tiled=True)  29.9 us
    scatter-add x2, other arithmetic, body(): slope = jnp.zeros((heads, total), jnp.float32).at[:, own_query].add(row_p...  18 us
  transfers between devices with their start and end apart: 3, of which 1 were waited for; matrix products, arithmetic and copies ran while one was open for 2% of the time, Pallas kernels for 0%

commit v1 on v0

v1 whole, which is shorter than its diff:
```python
import functools
import math

import jax
import jax.numpy as jnp
from jax import lax
from jax.experimental import pallas as pl
from jax.experimental.pallas import tpu as pltpu
from jax.sharding import PartitionSpec as P

MESH = pl.DeviceIdType.MESH
NEGATIVE = -1e30
LOG2E = 1.0 / math.log(2.0)
CHUNK = 128


def dot(a, b, dims):
    return lax.dot_general(a, b, (dims, ((), ())), preferred_element_type=jnp.float32)


def fold_rows(x):
    return jnp.sum(x.reshape(x.shape[0] // 8, 8, x.shape[1]), axis=0)


def fold_lanes(x):
    width = x.shape[1]
    out = x[:, 0:128]
    for k in range(128, width, 128):
        out = out + x[:, k : k + 128]
    return out


def lane_prefix(x):
    width = x.shape[1]
    lane = lax.broadcasted_iota(jnp.int32, x.shape, 1)
    shift = 1
    while shift < width:
        x = x + jnp.where(lane >= shift, pltpu.roll(x, shift, 1), 0.0)
        shift *= 2
    return x


def kernel(
    nb,
    na,
    heads,
    q_hbm,
    k_hbm,
    c_hbm,
    b_hbm,
    rate_ref,
    gc_ref,
    gb_ref,
    gr_ref,
    q_ref,
    k_ref,
    c_ref,
    b_ref,
    ch_ref,
    bt_ref,
    s_ref,
    w_ref,
    kcol_ref,
    rel_ref,
    scan_ref,
    rates_ref,
    stat_ref,
    fold_ref,
    colsend_ref,
    col_ref,
    slope_ref,
    gbown_ref,
    gbsend_ref,
    gbrecv_ref,
    gcown_ref,
    gcsend_ref,
    gcrecv_ref,
    in_sem,
    rate_send,
    rate_recv,
    stat_send,
    stat_recv,
    fold_send,
    fold_recv,
    col_send,
    col_recv,
    slope_send,
    slope_recv,
    gb_send,
    gb_recv,
    gc_send,
    gc_recv,
):
    pb = lax.axis_index("pb")
    ka = lax.axis_index("ka")
    qn, width = q_ref.shape
    kn = k_ref.shape[0]
    dh = width // heads
    state = c_ref.shape[1] // heads
    ratio = kn // qn
    steps = kn // CHUNK
    gb_rows = kn // nb
    gc_rows = qn // na
    per_chunk = CHUNK // gb_rows
    factor = 2.0 * qn * nb
    first = ratio * ka
    live = pb >= first
    plane_live = pb // ratio

    loads = [
        pltpu.make_async_copy(src, dst, in_sem.at[n])
        for n, (src, dst) in enumerate(
            ((q_hbm, q_ref), (k_hbm, k_ref), (c_hbm, c_ref), (b_hbm, b_ref))
        )
    ]
    for load in loads:
        load.start()

    rates_ref[...] = jnp.zeros_like(rates_ref)
    rates_ref[pb] = rate_ref[...]
    fold_ref[...] = jnp.zeros_like(fold_ref)
    slope_ref[...] = jnp.zeros_like(slope_ref)
    col_ref[...] = jnp.zeros_like(col_ref)
    stat_ref[...] = jnp.concatenate(
        [
            jnp.full((na, heads, qn), NEGATIVE, jnp.float32),
            jnp.zeros((na, heads, qn), jnp.float32),
        ],
        axis=1,
    )

    barrier = pltpu.get_barrier_semaphore()

    @pl.loop(1, na)
    def _(k):
        pl.semaphore_signal(
            barrier, inc=1, device_id=(pb, lax.rem(ka + k, na)), device_id_type=MESH
        )

    @pl.loop(1, nb)
    def _(k):
        pl.semaphore_signal(
            barrier, inc=1, device_id=(lax.rem(pb + k, nb), ka), device_id_type=MESH
        )

    def rate_copy(slot, target):
        return pltpu.make_async_remote_copy(
            src_ref=rates_ref.at[slot],
            dst_ref=rates_ref.at[slot],
            send_sem=rate_send.at[target],
            recv_sem=rate_recv.at[slot],
            device_id=(target, ka),
            device_id_type=MESH,
        )

    def stat_copy(slot, target):
        return pltpu.make_async_remote_copy(
            src_ref=stat_ref.at[slot],
            dst_ref=stat_ref.at[slot],
            send_sem=stat_send.at[target],
            recv_sem=stat_recv.at[slot],
            device_id=(pb, target),
            device_id_type=MESH,
        )

    def fold_copy(slot, target):
        return pltpu.make_async_remote_copy(
            src_ref=fold_ref.at[slot],
            dst_ref=fold_ref.at[slot],
            send_sem=fold_send.at[target],
            recv_sem=fold_recv.at[slot],
            device_id=(target, ka),
            device_id_type=MESH,
        )

    def col_copy(part, slot):
        return pltpu.make_async_remote_copy(
            src_ref=colsend_ref.at[part],
            dst_ref=col_ref.at[slot],
            send_sem=col_send.at[part],
            recv_sem=col_recv.at[slot],
            device_id=(first + part, ka),
            device_id_type=MESH,
        )

    def slope_copy(slot, target):
        return pltpu.make_async_remote_copy(
            src_ref=slope_ref.at[slot],
            dst_ref=slope_ref.at[slot],
            send_sem=slope_send.at[target],
            recv_sem=slope_recv.at[slot],
            device_id=(pb, target),
            device_id_type=MESH,
        )

    def gb_copy(slot, target):
        return pltpu.make_async_remote_copy(
            src_ref=gbsend_ref.at[target],
            dst_ref=gbrecv_ref.at[slot],
            send_sem=gb_send.at[target],
            recv_sem=gb_recv.at[slot],
            device_id=(target, ka),
            device_id_type=MESH,
        )

    def gc_copy(slot, target):
        return pltpu.make_async_remote_copy(
            src_ref=gcsend_ref.at[target],
            dst_ref=gcrecv_ref.at[slot],
            send_sem=gc_send.at[target],
            recv_sem=gc_recv.at[slot],
            device_id=(pb, target),
            device_id_type=MESH,
        )

    offset = pb * qn - ka * kn

    def mask_of(t):
        rows = lax.broadcasted_iota(jnp.int32, (CHUNK, qn), 0)
        cols = lax.broadcasted_iota(jnp.int32, (CHUNK, qn), 1)
        return cols - rows >= t * CHUNK - offset

    def chunk_rows(t):
        return pl.ds(pl.multiple_of(t * CHUNK, CHUNK), CHUNK)

    loads[0].wait()
    loads[1].wait()
    scale2 = LOG2E / math.sqrt(dh)

    @pl.when(live)
    def _():
        for h in range(heads):
            lanes = slice(h * dh, (h + 1) * dh)

            def score_turn(t, peak, h=h, lanes=lanes):
                s = dot(k_ref[chunk_rows(t), lanes], q_ref[:, lanes], ((1,), (1,)))
                s = jnp.where(mask_of(t), s * scale2, NEGATIVE)
                s_ref[h, chunk_rows(t), :] = s
                return jnp.maximum(peak, jnp.max(s.reshape(CHUNK // 8, 8, qn), axis=0))

            peak = lax.fori_loop(
                0, steps, score_turn, jnp.full((8, qn), NEGATIVE, jnp.float32)
            )
            peak = jnp.max(peak, axis=0, keepdims=True)

            def expo_turn(t, total, h=h, peak=peak):
                e = jnp.exp2(s_ref[h, chunk_rows(t), :] - peak)
                s_ref[h, chunk_rows(t), :] = e
                return total + fold_rows(e)

            total = lax.fori_loop(0, steps, expo_turn, jnp.zeros((8, qn), jnp.float32))
            stat_ref[ka, h : h + 1, :] = peak
            stat_ref[ka, heads + h : heads + h + 1, :] = jnp.sum(
                total, axis=0, keepdims=True
            )

    loads[2].wait()
    loads[3].wait()
    pl.semaphore_wait(barrier, na + nb - 2)

    @pl.when(live)
    def _():
        @pl.loop(1, na)
        def _(k):
            target = lax.rem(ka + k, na)

            @pl.when(target <= plane_live)
            def _():
                stat_copy(ka, target).start()

        @pl.loop(pb + 1, nb)
        def _(target):
            rate_copy(pb, target).start()

        head_of = lax.broadcasted_iota(jnp.int32, (qn, heads * state), 1) // state
        c_all = c_ref[...]
        for h in range(heads):
            ch_ref[h] = jnp.where(head_of == h, c_all, jnp.zeros_like(c_all))
        bt_ref[...] = jnp.transpose(b_ref[...])

        @pl.loop(first, pb)
        def _(slot):
            rate_copy(slot, slot).wait_recv()

        scan_ref[...] = jnp.zeros_like(scan_ref)
        scan_ref[0:heads, :] = rate_ref[...]
        for part in range(ratio):
            low = heads * (1 + part)
            scan_ref[low : low + heads, :] = rates_ref[first + part]
        rates = scan_ref[...]
        scan_ref[...] = lane_prefix(rates)
        ends = jnp.sum(rates, axis=1, keepdims=True)
        before = jnp.sum(
            jnp.sum(rates_ref[...], axis=0) - rate_ref[...], axis=1, keepdims=True
        )
        for part in range(ratio):
            pass
        for h in range(heads):
            shift = jnp.zeros((1, 1), jnp.float32)
            for part in range(ratio):
                row = heads * (1 + part) + h
                prefix = (scan_ref[row : row + 1, :] + shift) * LOG2E
                kcol_ref[h, part * qn : (part + 1) * qn, :] = jnp.transpose(
                    jnp.broadcast_to(prefix, (128, qn))
                )
                shift = shift + ends[row : row + 1, :]
        arow = (scan_ref[0:heads, :] + before) * LOG2E

        @pl.loop(0, plane_live + 1)
        def _(slot):
            @pl.when(slot != ka)
            def _():
                stat_copy(slot, slot).wait_recv()

        peaks = stat_ref[:, 0:heads, :]
        totals = stat_ref[:, heads : 2 * heads, :]
        peak = jnp.max(peaks, axis=0)
        total = jnp.sum(totals * jnp.exp2(peaks - peak[None]), axis=0)
        own_peak = stat_ref[ka, 0:heads, :]
        scaling = jnp.exp2(own_peak - peak) / total

        def grad_turn(n, row_sums):
            t = lax.rem(n + pb * gb_rows // CHUNK, steps)
            rows = chunk_rows(t)
            mask = mask_of(t)
            b_rows = b_ref[rows, :]
            out = jnp.zeros((CHUNK, heads * state), jnp.float32)
            new_sums = []
            for h in range(heads):
                inner = dot(b_rows, ch_ref[h], ((1,), (1,)))
                gap = jnp.concatenate(
                    [kcol_ref[h, rows, :]] * (qn // 128), axis=1
                ) - arow[h : h + 1, :]
                decay = jnp.exp2(jnp.where(mask, gap, NEGATIVE))
                student = inner * decay
                grad = student - s_ref[h, rows, :] * scaling[h : h + 1, :]
                weight = (grad * decay).astype(jnp.bfloat16)
                w_ref[h, rows, :] = weight
                related = grad * student
                rel_ref[h, rows, :] = fold_lanes(related)
                new_sums.append(row_sums[h] + fold_rows(related))
                out = out + dot(weight, ch_ref[h], ((1,), (0,)))
            out = out * factor
            for part in range(per_chunk):
                target = t * per_chunk + part
                piece = out[part * gb_rows : (part + 1) * gb_rows, :]
                gbsend_ref[target] = piece.astype(jnp.bfloat16)

                @pl.when(target == pb)
                def _(piece=piece):
                    gbown_ref[...] = piece

                @pl.when(target != pb)
                def _(target=target):
                    gb_copy(pb, target).start()

            return tuple(new_sums)

        row_sums = lax.fori_loop(
            0,
            steps,
            grad_turn,
            tuple(jnp.zeros((8, qn), jnp.float32) for _ in range(heads)),
        )

        fold = jnp.zeros((heads, 128), jnp.float32)
        for part in range(ratio):
            for h in range(heads):
                flipped = jnp.transpose(rel_ref[h, part * qn : (part + 1) * qn, :])
                sums = jnp.sum(flipped, axis=0, keepdims=True)
                colsend_ref[part, h : h + 1, :] = sums
            fold = fold + fold_lanes(colsend_ref[part])
        fold_ref[pb] = fold

        @pl.loop(first, pb)
        def _(target):
            fold_copy(pb, target).start()

        for part in range(ratio):

            @pl.when(pb != first + part)
            def _(part=part):
                col_copy(part, pb).start()

            @pl.when(pb == first + part)
            def _(part=part):
                col_ref[pb] = colsend_ref[part]

        for h in range(heads):
            slope_ref[ka, h : h + 1, 0:qn] = jnp.sum(
                row_sums[h], axis=0, keepdims=True
            )
            flat = dot(
                bt_ref[h * state : (h + 1) * state, :], w_ref[h], ((1,), (0,))
            )
            scan_t = jnp.transpose(flat * factor)
            gcown_ref[:, h * state : (h + 1) * state] = scan_t

        for target in range(na):
            gcsend_ref[target] = gcown_ref[
                target * gc_rows : (target + 1) * gc_rows, :
            ].astype(jnp.bfloat16)

        @pl.loop(1, na)
        def _(k):
            gc_copy(ka, lax.rem(ka + k, na)).start()

        @pl.loop(pb + 1, nb)
        def _(slot):
            fold_copy(slot, slot).wait_recv()

        slot_of = lax.broadcasted_iota(jnp.int32, (nb, 1, 1), 0)
        later = jnp.where(slot_of > pb, fold_ref[...], 0.0)
        slope_ref[ka, :, qn:] = jnp.sum(later, axis=0)

        @pl.when(plane_live == ka)
        def _():
            part = pb - first

            @pl.loop(first, nb)
            def _(slot):
                @pl.when(slot != pb)
                def _():
                    pltpu.make_async_remote_copy(
                        src_ref=colsend_ref.at[0],
                        dst_ref=col_ref.at[slot],
                        send_sem=col_send.at[0],
                        recv_sem=col_recv.at[slot],
                        device_id=(slot, ka),
                        device_id_type=MESH,
                    ).wait_recv()

            everything = jnp.sum(col_ref[...], axis=0)
            slope_ref[ka, :, 0:qn] = slope_ref[ka, :, 0:qn] - everything
            inside = fold_lanes(everything - col_ref[pb])

            @pl.when(part < ratio - 1)
            def _():
                slope_ref[ka, :, qn:] = inside

        @pl.loop(1, na)
        def _(k):
            slope_copy(ka, lax.rem(ka + k, na)).start()

    gc_ref[...] = jnp.zeros_like(gc_ref)

    @pl.when(live)
    def _():
        gc_ref[...] = gcown_ref[
            pl.ds(pl.multiple_of(ka * gc_rows, gc_rows), gc_rows), :
        ]

    @pl.loop(0, plane_live + 1)
    def _(slot):
        @pl.when(slot != ka)
        def _():
            gc_copy(slot, slot).wait_recv()
            gc_ref[...] += gcrecv_ref[slot].astype(jnp.float32)

    gb_ref[...] = jnp.zeros_like(gb_ref)

    @pl.when(live)
    def _():
        gb_ref[...] = gbown_ref[...]

    @pl.loop(first, nb)
    def _(slot):
        @pl.when(slot != pb)
        def _():
            gb_copy(slot, slot).wait_recv()
            gb_ref[...] += gbrecv_ref[slot].astype(jnp.float32)

    @pl.loop(0, plane_live + 1)
    def _(slot):
        @pl.when(slot != ka)
        def _():
            slope_copy(slot, slot).wait_recv()

    both = jnp.sum(slope_ref[...], axis=0)
    slope = both[:, 0:qn]
    after = jnp.sum(both[:, qn:], axis=1, keepdims=True)
    scan_ref[...] = jnp.zeros_like(scan_ref)
    scan_ref[0:heads, :] = slope
    suffix = jnp.sum(slope, axis=1, keepdims=True) - lane_prefix(scan_ref[...])[0:heads, :]
    gr_ref[...] = -factor * (suffix + slope + after)

    @pl.when(live)
    def _():
        @pl.loop(pb + 1, nb)
        def _(target):
            rate_copy(pb, target).wait_send()

        @pl.loop(first, pb)
        def _(target):
            fold_copy(pb, target).wait_send()

        for part in range(ratio):

            @pl.when(pb != first + part)
            def _(part=part):
                col_copy(part, pb).wait_send()

        @pl.loop(0, na)
        def _(target):
            @pl.when(target != ka)
            def _():
                @pl.when(target <= plane_live)
                def _():
                    stat_copy(ka, target).wait_send()

                gc_copy(ka, target).wait_send()
                slope_copy(ka, target).wait_send()

        @pl.loop(0, nb)
        def _(target):
            @pl.when(target != pb)
            def _():
                gb_copy(pb, target).wait_send()


def body(teacher_query, teacher_key, student_c, student_b, decay_rate):
    heads = decay_rate.shape[0]
    nb = lax.axis_size("pb")
    na = lax.axis_size("ka")
    qn, width = teacher_query.shape
    kn = teacher_key.shape[0]
    cols = student_c.shape[1]
    ratio = kn // qn
    f32, bf16 = jnp.float32, jnp.bfloat16
    vmem = pl.BlockSpec(memory_space=pltpu.VMEM)
    hbm = pl.BlockSpec(memory_space=pl.ANY)
    dma = pltpu.SemaphoreType.DMA
    scan_rows = -(-heads * (1 + ratio) // 8) * 8
    return pl.pallas_call(
        functools.partial(kernel, nb, na, heads),
        out_shape=(
            jax.ShapeDtypeStruct((qn // na, cols), f32),
            jax.ShapeDtypeStruct((kn // nb, cols), f32),
            jax.ShapeDtypeStruct((heads, qn), f32),
        ),
        in_specs=[hbm, hbm, hbm, hbm, vmem],
        out_specs=[vmem, vmem, vmem],
        scratch_shapes=[
            pltpu.VMEM((qn, width), bf16),
            pltpu.VMEM((kn, width), bf16),
            pltpu.VMEM((qn, cols), bf16),
            pltpu.VMEM((kn, cols), bf16),
            pltpu.VMEM((heads, qn, cols), bf16),
            pltpu.VMEM((cols, kn), bf16),
            pltpu.VMEM((heads, kn, qn), f32),
            pltpu.VMEM((heads, kn, qn), bf16),
            pltpu.VMEM((heads, kn, 128), f32),
            pltpu.VMEM((heads, kn, 128), f32),
            pltpu.VMEM((scan_rows, qn), f32),
            pltpu.VMEM((nb, heads, qn), f32),
            pltpu.VMEM((na, 2 * heads, qn), f32),
            pltpu.VMEM((nb, heads, 128), f32),
            pltpu.VMEM((ratio, heads, qn), f32),
            pltpu.VMEM((nb, heads, qn), f32),
            pltpu.VMEM((na, heads, qn + 128), f32),
            pltpu.VMEM((kn // nb, cols), f32),
            pltpu.VMEM((nb, kn // nb, cols), bf16),
            pltpu.VMEM((nb, kn // nb, cols), bf16),
            pltpu.VMEM((qn, cols), f32),
            pltpu.VMEM((na, qn // na, cols), bf16),
            pltpu.VMEM((na, qn // na, cols), bf16),
            dma((4,)),
            dma((nb,)),
            dma((nb,)),
            dma((na,)),
            dma((na,)),
            dma((nb,)),
            dma((nb,)),
            dma((ratio,)),
            dma((nb,)),
            dma((na,)),
            dma((na,)),
            dma((nb,)),
            dma((nb,)),
            dma((na,)),
            dma((na,)),
        ],
        compiler_params=pltpu.CompilerParams(
            collective_id=0, has_side_effects=True, vmem_limit_bytes=48 * 1024 * 1024
        ),
    )(teacher_query, teacher_key, student_c, student_b, decay_rate)


def solution(mesh):
    placed = (P("pb", None), P("ka", None), P("pb", None), P("ka", None), P(None, "pb"))
    return jax.shard_map(
        body,
        mesh=mesh,
        in_specs=placed,
        out_specs=(P(("pb", "ka"), None), P(("ka", "pb"), None), P(None, "pb")),
        check_vma=False,
    )
```

time: 748 us -> 61.9 us (0.08)
  the two profiles are of different devices: /device:TPU:1 before, /device:TPU:32 now
where the time goes in v1:
time: 61.9 us; the launch traced here: 61.6 us
  Pallas kernels  54.6 us (88%)
  local copies, waits for them, and re-layouts  6.33 us (10%)
  between operations  0.65 us (1%)
    pallas_call x1, Pallas kernels, body(): pl.pallas_call(functools.partial(kernel, nb, na, heads), out_shape=(jax.S...  54.6 us
    unnamed x13, local copies, waits for them, and re-layouts  6.33 us

profile of v1, /device:TPU:32, one launch (start us, length us, event | category | flops | bytes accessed | tf_op | source)
XLA Modules:
  0.0 61.6 jit_solution(3611347721277809878)
XLA Ops:
  0.6 0.0 copy-start
  0.6 1.0 %copy-done = bf16[1024,256]{1,0:T(8,128)(2,1)S(1)} copy-done((bf16[1024,256]{1,0:T(8,128)(2,1)S(1)}, bf16[1024,256]{1,0:T(8,128)(2,1)}, u32[]{:S(2)}) %copy-start) | copy-done | bytes 524312
  1.7 0.0 copy-start.1
  1.7 0.9 %copy-done.1 = bf16[512,256]{1,0:T(8,128)(2,1)S(1)} copy-done((bf16[512,256]{1,0:T(8,128)(2,1)S(1)}, bf16[512,256]{1,0:T(8,128)(2,1)}, u32[]{:S(2)}) %copy-start.1) | copy-done | bytes 262168
  2.6 0.0 copy-start.2
  2.6 0.9 %copy-done.2 = bf16[1024,128]{1,0:T(8,128)(2,1)S(1)} copy-done((bf16[1024,128]{1,0:T(8,128)(2,1)S(1)}, bf16[1024,128]{1,0:T(8,128)(2,1)}, u32[]{:S(2)}) %copy-start.2) | copy-done | bytes 262168
  3.6 0.0 copy-start.3
  3.6 0.9 %copy-done.3 = bf16[512,128]{1,0:T(8,128)(2,1)S(1)} copy-done((bf16[512,128]{1,0:T(8,128)(2,1)S(1)}, bf16[512,128]{1,0:T(8,128)(2,1)}, u32[]{:S(2)}) %copy-start.3) | copy-done | bytes 131096
  4.5 0.0 copy-start.4
  4.5 0.7 %copy-done.4 = f32[2,512]{1,0:T(2,128)S(1)} copy-done((f32[2,512]{1,0:T(2,128)S(1)}, f32[2,512]{1,0:T(2,128)}, u32[]{:S(2)}) %copy-start.4) | copy-done | bytes 4120
  5.2 54.6 %shard_map.76 = (f32[32,128]{1,0:T(8,128)S(1)}, f32[32,128]{1,0:T(8,128)S(1)}, f32[2,512]{1,0:T(2,128)S(1)}) custom-call(bf16[512,256]{1,0:T(8,128)(2,1)S(1)} %copy-done.1, bf16[1024,256]{1,0:T(8,128)(2,1)S(1)} %copy-done, bf16[512,128]{1,0:T(8,128)(2,1)S(1)} %copy-done.3, bf16[1024,128]{1,0:T(8,128)(2,1)S(1)} %copy-done.2, f32[2,512]{1,0:T(2,128)S(1)} %copy-done.4), custom_call_target="tpu_custom_call" | custom-call | tf_op jit(solution)/shard_map/pallas_call | solution.py:534
  59.8 0.6 copy.11
  60.4 0.6 copy.12
  61.0 0.6 copy.13
Async XLA Ops:
  0.6 1.0 %copy-start = (bf16[1024,256]{1,0:T(8,128)(2,1)S(1)}, bf16[1024,256]{1,0:T(8,128)(2,1)}, u32[]{:S(2)}) copy-start(bf16[1024,256]{1,0:T(8,128)(2,1)} %k_hbm.1) | copy-start | bytes 1572868
  1.7 0.9 %copy-start.1 = (bf16[512,256]{1,0:T(8,128)(2,1)S(1)}, bf16[512,256]{1,0:T(8,128)(2,1)}, u32[]{:S(2)}) copy-start(bf16[512,256]{1,0:T(8,128)(2,1)} %q_hbm.1) | copy-start | bytes 786436
  2.6 0.9 %copy-start.2 = (bf16[1024,128]{1,0:T(8,128)(2,1)S(1)}, bf16[1024,128]{1,0:T(8,128)(2,1)}, u32[]{:S(2)}) copy-start(bf16[1024,128]{1,0:T(8,128)(2,1)} %b_hbm.1) | copy-start | bytes 786436
  3.6 0.9 %copy-start.3 = (bf16[512,128]{1,0:T(8,128)(2,1)S(1)}, bf16[512,128]{1,0:T(8,128)(2,1)}, u32[]{:S(2)}) copy-start(bf16[512,128]{1,0:T(8,128)(2,1)} %c_hbm.1) | copy-start | bytes 393220
  4.5 0.7 %copy-start.4 = (f32[2,512]{1,0:T(2,128)S(1)}, f32[2,512]{1,0:T(2,128)}, u32[]{:S(2)}) copy-start(f32[2,512]{1,0:T(2,128)} %rate_ref.1) | copy-start | bytes 12292

commit v2 on v1

v2 whole, which is shorter than its diff:
```python
import functools
import math

import jax
import jax.numpy as jnp
from jax import lax
from jax.experimental import pallas as pl
from jax.experimental.pallas import tpu as pltpu
from jax.sharding import PartitionSpec as P

MESH = pl.DeviceIdType.MESH
NEGATIVE = -1e30
LOG2E = 1.0 / math.log(2.0)
CHUNK = 128


def dot(a, b, dims):
    return lax.dot_general(a, b, (dims, ((), ())), preferred_element_type=jnp.float32)


def fold_rows(x):
    return jnp.sum(x.reshape(x.shape[0] // 8, 8, x.shape[1]), axis=0)


def fold_lanes(x):
    width = x.shape[1]
    out = x[:, 0:128]
    for k in range(128, width, 128):
        out = out + x[:, k : k + 128]
    return out


def lane_prefix(x):
    width = x.shape[1]
    lane = lax.broadcasted_iota(jnp.int32, x.shape, 1)
    shift = 1
    while shift < width:
        x = x + jnp.where(lane >= shift, pltpu.roll(x, shift, 1), 0.0)
        shift *= 2
    return x


def kernel(
    nb,
    na,
    heads,
    q_hbm,
    k_hbm,
    c_hbm,
    b_hbm,
    rate_hbm,
    gc_ref,
    gb_ref,
    gr_ref,
    q_ref,
    k_ref,
    c_ref,
    b_ref,
    ch_ref,
    bt_ref,
    s_ref,
    w_ref,
    kcol_ref,
    scan_ref,
    pair_ref,
    krate_ref,
    rfold_ref,
    stat_ref,
    cs_ref,
    cssib_ref,
    fold_ref,
    colsend_ref,
    col_ref,
    slope_ref,
    gbpart_ref,
    gbsib_ref,
    gbown_ref,
    gbsend_ref,
    gbrecv_ref,
    gcown_ref,
    gcsend_ref,
    gcrecv_ref,
    in_sem,
    pair_send,
    pair_recv,
    rate_send,
    krate_recv,
    rfold_recv,
    stat_send,
    stat_recv,
    cs_send,
    cs_recv,
    fold_send,
    fold_recv,
    col_send,
    col_recv,
    slope_send,
    slope_recv,
    gx_send,
    gx_recv,
    gb_send,
    gb_recv,
    gc_send,
    gc_recv,
):
    pb = lax.axis_index("pb")
    ka = lax.axis_index("ka")
    qn, width = q_ref.shape
    kn = k_ref.shape[0]
    dh = width // heads
    cols = c_ref.shape[1]
    state = cols // heads
    nz = nb // 2
    z = pb // 2
    core = lax.rem(pb, 2)
    other = 1 - core
    sibling = 2 * z + other
    steps = kn // CHUNK
    half = steps // 2
    gb_rows = kn // nb
    gc_rows = qn // na
    per_chunk = CHUNK // (2 * gb_rows)
    factor = 2.0 * qn * nb
    live = z >= ka
    diagonal = z == ka

    loads = [
        pltpu.make_async_copy(src, dst, in_sem.at[n])
        for n, (src, dst) in enumerate(
            (
                (q_hbm, q_ref),
                (k_hbm, k_ref),
                (rate_hbm, pair_ref.at[core]),
                (c_hbm, c_ref),
                (b_hbm, b_ref),
            )
        )
    ]
    for load in loads:
        load.start()

    barrier = pltpu.get_barrier_semaphore()
    pl.semaphore_signal(barrier, inc=1, device_id=(sibling, ka), device_id_type=MESH)

    @pl.loop(1, na)
    def _(k):
        pl.semaphore_signal(
            barrier, inc=1, device_id=(pb, lax.rem(ka + k, na)), device_id_type=MESH
        )

    @pl.loop(1, nz)
    def _(k):
        pl.semaphore_signal(
            barrier,
            inc=1,
            device_id=(2 * lax.rem(z + k, nz) + core, ka),
            device_id_type=MESH,
        )

    def to(src, dst, send, recv, device):
        return pltpu.make_async_remote_copy(
            src_ref=src,
            dst_ref=dst,
            send_sem=send,
            recv_sem=recv,
            device_id=device,
            device_id_type=MESH,
        )

    def up(target):
        return (2 * target + core, ka)

    def pair_copy(slot):
        return to(
            pair_ref.at[slot], pair_ref.at[slot], pair_send, pair_recv, (sibling, ka)
        )

    def krate_copy(target):
        return to(pair_ref, krate_ref, rate_send.at[target], krate_recv, up(target))

    def rfold_copy(slot, target):
        return to(
            rfold_ref.at[slot],
            rfold_ref.at[slot],
            rate_send.at[target],
            rfold_recv.at[slot],
            up(target),
        )

    def stat_copy(slot, target):
        return to(
            stat_ref.at[slot],
            stat_ref.at[slot],
            stat_send.at[target],
            stat_recv.at[slot],
            (pb, target),
        )

    def cs_copy():
        return to(cs_ref, cssib_ref, cs_send, cs_recv, (sibling, ka))

    def fold_copy(slot, target):
        return to(
            fold_ref.at[slot],
            fold_ref.at[slot],
            fold_send.at[target],
            fold_recv.at[slot],
            up(target),
        )

    def col_copy(slot):
        return to(
            colsend_ref, col_ref.at[slot], col_send, col_recv.at[slot], up(ka)
        )

    def slope_copy(slot, target):
        return to(
            slope_ref.at[slot],
            slope_ref.at[slot],
            slope_send,
            slope_recv.at[slot],
            (pb, target),
        )

    def gx_copy(start, count):
        return to(
            gbpart_ref.at[pl.ds(start, count), other],
            gbsib_ref.at[pl.ds(start, count)],
            gx_send,
            gx_recv,
            (sibling, ka),
        )

    def gb_copy(slot, target):
        return to(
            gbsend_ref.at[target],
            gbrecv_ref.at[slot],
            gb_send,
            gb_recv.at[slot],
            up(target),
        )

    def gc_copy(slot, target):
        return to(
            gcsend_ref.at[target],
            gcrecv_ref.at[slot],
            gc_send,
            gc_recv.at[slot],
            (pb, target),
        )

    offset = pb * qn - ka * kn

    def mask_of(t):
        rows = lax.broadcasted_iota(jnp.int32, (CHUNK, qn), 0)
        lanes = lax.broadcasted_iota(jnp.int32, (CHUNK, qn), 1)
        return lanes - rows >= t * CHUNK - offset

    def chunk_rows(t):
        return pl.ds(pl.multiple_of(t * CHUNK, CHUNK), CHUNK)

    scale2 = LOG2E / math.sqrt(dh)

    def head_stats(h):
        lanes = slice(h * dh, (h + 1) * dh)

        def score_turn(t, peak):
            s = dot(k_ref[chunk_rows(t), lanes], q_ref[:, lanes], ((1,), (1,)))
            s = jnp.where(mask_of(t), s * scale2, NEGATIVE)
            s_ref[h, chunk_rows(t), :] = s
            return jnp.maximum(peak, jnp.max(s.reshape(CHUNK // 8, 8, qn), axis=0))

        peak = lax.fori_loop(
            0, steps, score_turn, jnp.full((8, qn), NEGATIVE, jnp.float32)
        )
        peak = jnp.max(peak, axis=0, keepdims=True)

        def expo_turn(t, total):
            e = jnp.exp2(s_ref[h, chunk_rows(t), :] - peak)
            s_ref[h, chunk_rows(t), :] = e
            return total + fold_rows(e)

        total = lax.fori_loop(0, steps, expo_turn, jnp.zeros((8, qn), jnp.float32))
        stat_ref[ka, h : h + 1, :] = peak
        stat_ref[ka, heads + h : heads + h + 1, :] = jnp.sum(
            total, axis=0, keepdims=True
        )

    @pl.when(live)
    def _():
        stat_init = jnp.concatenate(
            [
                jnp.full((heads, qn), NEGATIVE, jnp.float32),
                jnp.zeros((heads, qn), jnp.float32),
            ],
            axis=0,
        )

        @pl.loop(z + 1, na)
        def _(slot):
            stat_ref[slot] = stat_init

    loads[0].wait()
    loads[1].wait()

    @pl.when(live)
    def _():
        for h in range(heads // 2):
            head_stats(h)

    for load in loads[2:]:
        load.wait()
    pl.semaphore_wait(barrier, na + nz - 1)

    @pl.when(live)
    def _():
        pair_copy(core).start()
        for h in range(heads // 2, heads):
            head_stats(h)

        @pl.loop(1, na)
        def _(k):
            target = lax.rem(ka + k, na)

            @pl.when(target <= z)
            def _():
                stat_copy(ka, target).start()

        pair_copy(other).wait_recv()
        own_fold = jnp.stack([fold_lanes(pair_ref[0]), fold_lanes(pair_ref[1])])
        rfold_ref[z] = own_fold

        @pl.loop(z + 1, nz)
        def _(target):
            @pl.when(diagonal)
            def _():
                krate_copy(target).start()

            @pl.when(jnp.logical_not(diagonal))
            def _():
                rfold_copy(z, target).start()

        head_of = lax.broadcasted_iota(jnp.int32, (qn, cols), 1) // state
        c_all = c_ref[...]
        for h in range(heads):
            ch_ref[h] = jnp.where(head_of == h, c_all, jnp.zeros_like(c_all))
        bt_ref[...] = jnp.transpose(b_ref[...])

        scan_ref[...] = jnp.zeros_like(scan_ref)
        scan_ref[0:heads, :] = pair_ref[core]

        @pl.when(diagonal)
        def _():
            for part in range(2):
                low = heads * (1 + part)
                scan_ref[low : low + heads, :] = pair_ref[part]

        @pl.when(jnp.logical_not(diagonal))
        def _():
            krate_copy(z).wait_recv()
            for part in range(2):
                low = heads * (1 + part)
                scan_ref[low : low + heads, :] = krate_ref[part]

        rates = scan_ref[...]
        scan_ref[...] = lane_prefix(rates)
        ends = jnp.sum(rates, axis=1, keepdims=True)
        for h in range(heads):
            shift = jnp.zeros((1, 1), jnp.float32)
            for part in range(2):
                row = heads * (1 + part) + h
                prefix = (scan_ref[row : row + 1, :] + shift) * LOG2E
                kcol_ref[h, part * qn : (part + 1) * qn, :] = jnp.transpose(
                    jnp.broadcast_to(prefix, (128, qn))
                )
                shift = shift + ends[row : row + 1, :]

        def between_turn(slot, total):
            rfold_copy(slot, z).wait_recv()
            return total + rfold_ref[slot, 0] + rfold_ref[slot, 1]

        between = lax.fori_loop(
            ka + 1, z, between_turn, jnp.zeros((heads, 128), jnp.float32)
        )
        between = between + jnp.where(core == 1, rfold_ref[z, 0], 0.0)
        before = jnp.sum(between, axis=1, keepdims=True) + jnp.where(
            diagonal, 0.0, ends[heads : 2 * heads] + ends[2 * heads : 3 * heads]
        )
        arow = (scan_ref[0:heads, :] + before) * LOG2E

        @pl.loop(0, z + 1)
        def _(slot):
            @pl.when(slot != ka)
            def _():
                stat_copy(slot, slot).wait_recv()

        peaks = stat_ref[:, 0:heads, :]
        totals = stat_ref[:, heads : 2 * heads, :]
        peak = jnp.max(peaks, axis=0)
        total = jnp.sum(totals * jnp.exp2(peaks - peak[None]), axis=0)
        own_peak = stat_ref[ka, 0:heads, :]
        scaling = jnp.exp2(own_peak - peak) / total

        def grad_turn(t, row_sums):
            rows = chunk_rows(t)
            mask = mask_of(t)
            b_rows = b_ref[rows, :]
            out = jnp.zeros((CHUNK, cols), jnp.float32)
            new_sums = []
            for h in range(heads):
                inner = dot(b_rows, ch_ref[h], ((1,), (1,)))
                gap = jnp.concatenate(
                    [kcol_ref[h, rows, :]] * (qn // 128), axis=1
                ) - arow[h : h + 1, :]
                decay = jnp.exp2(jnp.where(mask, gap, NEGATIVE))
                student = inner * decay
                grad = student - s_ref[h, rows, :] * scaling[h : h + 1, :]
                weight = (grad * decay).astype(jnp.bfloat16)
                w_ref[h, rows, :] = weight
                related = grad * student
                flipped = jnp.transpose(fold_lanes(related))
                cs_ref[t, h : h + 1, :] = jnp.sum(flipped, axis=0, keepdims=True)
                new_sums.append(row_sums[h] + fold_rows(related))
                out = out + dot(weight, ch_ref[h], ((1,), (0,)))
            gbpart_ref[pl.ds(t * per_chunk, per_chunk)] = (out * factor).reshape(
                per_chunk, 2, gb_rows, cols
            )
            gx_copy(t * per_chunk, per_chunk).start()
            return tuple(new_sums)

        row_sums = lax.fori_loop(
            0,
            steps,
            grad_turn,
            tuple(jnp.zeros((8, qn), jnp.float32) for _ in range(heads)),
        )
        cs_copy().start()

        for h in range(heads):
            slope_ref[ka, h : h + 1, 0:qn] = jnp.sum(
                row_sums[h], axis=0, keepdims=True
            )
            flat = dot(
                bt_ref[h * state : (h + 1) * state, :], w_ref[h], ((1,), (0,))
            )
            gcown_ref[:, h * state : (h + 1) * state] = jnp.transpose(flat * factor)

        gcsend_ref[...] = (
            gcown_ref[...].reshape(na, gc_rows, cols).astype(jnp.bfloat16)
        )

        cs_copy().wait_recv()
        sib_fold = jnp.sum(cssib_ref[...], axis=0)
        fold_ref[z] = jnp.sum(cs_ref[...], axis=0) + sib_fold
        mine = pl.ds(core * half, half)
        colsend_ref[...] = cs_ref[mine] + cssib_ref[mine]

        @pl.when(jnp.logical_not(diagonal))
        def _():
            col_copy(z).start()

        @pl.loop(ka, z)
        def _(target):
            fold_copy(z, target).start()

        @pl.loop(1, na)
        def _(k):
            gc_copy(ka, lax.rem(ka + k, na)).start()

        gx_copy(0, nz).wait_recv()

        @pl.loop(1, nz)
        def _(k):
            target = lax.rem(z + k, nz)
            gbsend_ref[target] = (
                gbpart_ref[target, core] + gbsib_ref[target]
            ).astype(jnp.bfloat16)
            gb_copy(z, target).start()

        gbown_ref[...] = gbpart_ref[z, core] + gbsib_ref[z]

        def later_turn(slot, total):
            fold_copy(slot, z).wait_recv()
            return total + fold_ref[slot]

        later = lax.fori_loop(
            z + 1, nz, later_turn, jnp.where(core == 0, sib_fold, 0.0)
        )
        slope_ref[ka, :, qn:] = later

        @pl.when(diagonal)
        def _():
            def col_turn(slot, total):
                col_copy(slot).wait_recv()
                return total + col_ref[slot]

            above = lax.fori_loop(
                z + 1, nz, col_turn, jnp.zeros(colsend_ref.shape, jnp.float32)
            )
            everything = above + colsend_ref[...]
            for k in range(half):
                lanes = slice(k * CHUNK, (k + 1) * CHUNK)
                slope_ref[ka, :, lanes] = slope_ref[ka, :, lanes] - everything[k]

            @pl.when(core == 0)
            def _():
                slope_ref[ka, :, qn:] = jnp.sum(above + cssib_ref[mine], axis=0)

        @pl.loop(1, na)
        def _(k):
            slope_copy(ka, lax.rem(ka + k, na)).start()

    @pl.when(live)
    def _():
        gc_ref[...] = gcown_ref[
            pl.ds(pl.multiple_of(ka * gc_rows, gc_rows), gc_rows), :
        ]
        gb_ref[...] = gbown_ref[...]

    @pl.when(jnp.logical_not(live))
    def _():
        gc_ref[...] = jnp.zeros_like(gc_ref)
        gb_ref[...] = jnp.zeros_like(gb_ref)

    def gc_turn(slot, total):
        gc_copy(slot, slot).wait_recv()
        return total + gcrecv_ref[slot].astype(jnp.float32)

    sums = lax.fori_loop(0, jnp.minimum(ka, z + 1), gc_turn, gc_ref[...])
    gc_ref[...] = lax.fori_loop(ka + 1, z + 1, gc_turn, sums)

    def gb_turn(slot, total):
        gb_copy(slot, slot).wait_recv()
        return total + gbrecv_ref[slot].astype(jnp.float32)

    sums = lax.fori_loop(ka, z, gb_turn, gb_ref[...])
    gb_ref[...] = lax.fori_loop(jnp.maximum(ka, z + 1), nz, gb_turn, sums)

    @pl.when(live)
    def _():
        pair_copy(core).wait_send()
        gx_copy(0, nz).wait_send()
        cs_copy().wait_send()

        @pl.when(jnp.logical_not(diagonal))
        def _():
            col_copy(z).wait_send()

        @pl.loop(z + 1, nz)
        def _(target):
            @pl.when(diagonal)
            def _():
                krate_copy(target).wait_send()

            @pl.when(jnp.logical_not(diagonal))
            def _():
                rfold_copy(z, target).wait_send()

        @pl.loop(ka, z)
        def _(target):
            fold_copy(z, target).wait_send()

        @pl.loop(0, z + 1)
        def _(target):
            @pl.when(target != ka)
            def _():
                stat_copy(ka, target).wait_send()

        rest = pl.ds(0, na - 1)
        to(gcsend_ref.at[rest], gcrecv_ref.at[rest], gc_send, gc_recv.at[0], (pb, ka)).wait_send()
        rest = pl.ds(0, nz - 1)
        to(gbsend_ref.at[rest], gbrecv_ref.at[rest], gb_send, gb_recv.at[0], (pb, ka)).wait_send()

    def slope_turn(slot, total):
        slope_copy(slot, slot).wait_recv()
        return total + slope_ref[slot]

    @pl.when(jnp.logical_not(live))
    def _():
        slope_ref[ka] = jnp.zeros(slope_ref.shape[1:], jnp.float32)

    both = lax.fori_loop(0, jnp.minimum(ka, z + 1), slope_turn, slope_ref[ka])
    both = lax.fori_loop(ka + 1, z + 1, slope_turn, both)
    slope = both[:, 0:qn]
    after = jnp.sum(both[:, qn:], axis=1, keepdims=True)
    scan_ref[...] = jnp.zeros_like(scan_ref)
    scan_ref[0:heads, :] = slope
    suffix = jnp.sum(slope, axis=1, keepdims=True) - lane_prefix(scan_ref[...])[0:heads, :]
    gr_ref[...] = -factor * (suffix + slope + after)

    @pl.when(live)
    def _():
        rest = pl.ds(0, na - 1)
        to(slope_ref.at[rest], slope_ref.at[rest], slope_send, slope_recv.at[0], (pb, ka)).wait_send()


def body(teacher_query, teacher_key, student_c, student_b, decay_rate):
    heads = decay_rate.shape[0]
    nb = lax.axis_size("pb")
    na = lax.axis_size("ka")
    qn, width = teacher_query.shape
    kn = teacher_key.shape[0]
    cols = student_c.shape[1]
    nz = nb // 2
    steps = kn // CHUNK
    f32, bf16 = jnp.float32, jnp.bfloat16
    vmem = pl.BlockSpec(memory_space=pltpu.VMEM)
    hbm = pl.BlockSpec(memory_space=pl.ANY)
    dma = pltpu.SemaphoreType.DMA
    scan_rows = -(-heads * 3 // 8) * 8
    return pl.pallas_call(
        functools.partial(kernel, nb, na, heads),
        out_shape=(
            jax.ShapeDtypeStruct((qn // na, cols), f32),
            jax.ShapeDtypeStruct((kn // nb, cols), f32),
            jax.ShapeDtypeStruct((heads, qn), f32),
        ),
        in_specs=[hbm, hbm, hbm, hbm, hbm],
        out_specs=[vmem, vmem, vmem],
        scratch_shapes=[
            pltpu.VMEM((qn, width), bf16),
            pltpu.VMEM((kn, width), bf16),
            pltpu.VMEM((qn, cols), bf16),
            pltpu.VMEM((kn, cols), bf16),
            pltpu.VMEM((heads, qn, cols), bf16),
            pltpu.VMEM((cols, kn), bf16),
            pltpu.VMEM((heads, kn, qn), f32),
            pltpu.VMEM((heads, kn, qn), bf16),
            pltpu.VMEM((heads, kn, 128), f32),
            pltpu.VMEM((scan_rows, qn), f32),
            pltpu.VMEM((2, heads, qn), f32),
            pltpu.VMEM((2, heads, qn), f32),
            pltpu.VMEM((nz, 2, heads, 128), f32),
            pltpu.VMEM((na, 2 * heads, qn), f32),
            pltpu.VMEM((steps, heads, CHUNK), f32),
            pltpu.VMEM((steps, heads, CHUNK), f32),
            pltpu.VMEM((nz, heads, CHUNK), f32),
            pltpu.VMEM((steps // 2, heads, CHUNK), f32),
            pltpu.VMEM((nz, steps // 2, heads, CHUNK), f32),
            pltpu.VMEM((na, heads, qn + 128), f32),
            pltpu.VMEM((nz, 2, kn // nb, cols), f32),
            pltpu.VMEM((nz, kn // nb, cols), f32),
            pltpu.VMEM((kn // nb, cols), f32),
            pltpu.VMEM((nz, kn // nb, cols), bf16),
            pltpu.VMEM((nz, kn // nb, cols), bf16),
            pltpu.VMEM((qn, cols), f32),
            pltpu.VMEM((na, qn // na, cols), bf16),
            pltpu.VMEM((na, qn // na, cols), bf16),
            dma((5,)),
            dma,
            dma,
            dma((nz,)),
            dma,
            dma((nz,)),
            dma((na,)),
            dma((na,)),
            dma,
            dma,
            dma((nz,)),
            dma((nz,)),
            dma,
            dma((nz,)),
            dma,
            dma((na,)),
            dma,
            dma,
            dma,
            dma((nz,)),
            dma,
            dma((na,)),
        ],
        compiler_params=pltpu.CompilerParams(
            collective_id=0, has_side_effects=True, vmem_limit_bytes=62 * 1024 * 1024
        ),
    )(teacher_query, teacher_key, student_c, student_b, decay_rate)


def solution(mesh):
    placed = (P("pb", None), P("ka", None), P("pb", None), P("ka", None), P(None, "pb"))
    return jax.shard_map(
        body,
        mesh=mesh,
        in_specs=placed,
        out_specs=(P(("pb", "ka"), None), P(("ka", "pb"), None), P(None, "pb")),
        check_vma=False,
    )
```

time: 61.9 us -> 50.2 us (0.81)
  the two profiles are of different devices: /device:TPU:32 before, /device:TPU:1 now
where the time goes in v2:
time: 50.2 us; the launch traced here: 50 us
  Pallas kernels  46.7 us (93%)
  local copies, waits for them, and re-layouts  2.6 us (5%)
  between operations  0.65 us (1%)
    pallas_call x1, Pallas kernels, body(): pl.pallas_call(functools.partial(kernel, nb, na, heads), out_shape=(jax.S...  46.7 us
    unnamed x7, local copies, waits for them, and re-layouts  2.6 us

profile of v2, /device:TPU:1, one launch (start us, length us, event | category | flops | bytes accessed | tf_op | source)
XLA Modules:
  0.0 50.0 jit_solution(585162152928508555)
XLA Ops:
  0.6 46.7 %shard_map.76 = (f32[32,128]{1,0:T(8,128)}, f32[32,128]{1,0:T(8,128)}, f32[2,512]{1,0:T(2,128)}) custom-call(bf16[512,256]{1,0:T(8,128)(2,1)} %q_hbm.1, bf16[1024,256]{1,0:T(8,128)(2,1)} %k_hbm.1, bf16[512,128]{1,0:T(8,128)(2,1)} %c_hbm.1, bf16[1024,128]{1,0:T(8,128)(2,1)} %b_hbm.1, f32[2,512]{1,0:T(2,128)} %rate_hbm.1), custom_call_target="tpu_custom_call" | custom-call | tf_op jit(solution)/shard_map/pallas_call | solution.py:611
  47.4 0.0 copy-start
  47.4 1.3 %copy.11 = f32[32,128]{1,0:T(8,128)} copy(f32[32,128]{1,0:T(8,128)} %get-tuple-element.6) | data formatting | bytes 32768
  48.7 0.0 copy-done
  48.7 0.0 copy-start.1
  48.7 0.6 %copy.12 = f32[32,128]{1,0:T(8,128)} copy(f32[32,128]{1,0:T(8,128)S(1)} %copy-done) | data formatting | bytes 32768
  49.3 0.1 copy-done.1
  49.4 0.6 %copy.13 = f32[2,512]{1,0:T(2,128)} copy(f32[2,512]{1,0:T(2,128)S(1)} %copy-done.1) | data formatting | bytes 8192
Async XLA Ops:
  47.4 1.3 %copy-start = (f32[32,128]{1,0:T(8,128)S(1)}, f32[32,128]{1,0:T(8,128)}, u32[]{:S(2)}) copy-start(f32[32,128]{1,0:T(8,128)} %get-tuple-element.7) | copy-start | bytes 49156
  48.7 0.7 %copy-start.1 = (f32[2,512]{1,0:T(2,128)S(1)}, f32[2,512]{1,0:T(2,128)}, u32[]{:S(2)}) copy-start(f32[2,512]{1,0:T(2,128)} %get-tuple-element.8) | copy-start | bytes 12292

commit v3 on v2

--- a/solution.py
+++ b/solution.py
@@ -11,7 +11,8 @@
 MESH = pl.DeviceIdType.MESH
 NEGATIVE = -1e30
 LOG2E = 1.0 / math.log(2.0)
-CHUNK = 128
+CHUNK = 256
+PIECE = 16
 
 
 def dot(a, b, dims):
@@ -72,6 +73,8 @@
     colsend_ref,
     col_ref,
     slope_ref,
+    rs_ref,
+    gct_ref,
     gbpart_ref,
     gbsib_ref,
     gbown_ref,
@@ -116,7 +119,9 @@
     other = 1 - core
     sibling = 2 * z + other
     steps = kn // CHUNK
-    half = steps // 2
+    half = qn // 128
+    pieces = CHUNK // PIECE
+    blocks = CHUNK // 128
     gb_rows = kn // nb
     gc_rows = qn // na
     per_chunk = CHUNK // (2 * gb_rows)
@@ -227,7 +232,7 @@
             gbpart_ref.at[pl.ds(start, count), other],
             gbsib_ref.at[pl.ds(start, count)],
             gx_send,
-            gx_recv,
+            gx_recv.at[start // per_chunk],
             (sibling, ka),
         )
 
@@ -251,24 +256,32 @@
 
     offset = pb * qn - ka * kn
 
-    def mask_of(t):
-        rows = lax.broadcasted_iota(jnp.int32, (CHUNK, qn), 0)
-        lanes = lax.broadcasted_iota(jnp.int32, (CHUNK, qn), 1)
-        return lanes - rows >= t * CHUNK - offset
+    def mask_of(t, piece):
+        rows = lax.broadcasted_iota(jnp.int32, (PIECE, qn), 0)
+        lanes = lax.broadcasted_iota(jnp.int32, (PIECE, qn), 1)
+        return lanes - rows >= t * CHUNK + piece * PIECE - offset
+
+    def piece_rows(t, piece):
+        return pl.ds(pl.multiple_of(t * CHUNK + piece * PIECE, PIECE), PIECE)
 
     def chunk_rows(t):
         return pl.ds(pl.multiple_of(t * CHUNK, CHUNK), CHUNK)
 
     scale2 = LOG2E / math.sqrt(dh)
 
-    def head_stats(h):
+    def head_stats(h, masked):
         lanes = slice(h * dh, (h + 1) * dh)
 
         def score_turn(t, peak):
             s = dot(k_ref[chunk_rows(t), lanes], q_ref[:, lanes], ((1,), (1,)))
-            s = jnp.where(mask_of(t), s * scale2, NEGATIVE)
-            s_ref[h, chunk_rows(t), :] = s
-            return jnp.maximum(peak, jnp.max(s.reshape(CHUNK // 8, 8, qn), axis=0))
+            for n in range(pieces):
+                part = s[n * PIECE : (n + 1) * PIECE] * scale2
+                if masked:
+                    part = jnp.where(mask_of(t, n), part, NEGATIVE)
+                s_ref[h, piece_rows(t, n), :] = part
+                for k in range(0, PIECE, 8):
+                    peak = jnp.maximum(peak, part[k : k + 8])
+            return peak
 
         peak = lax.fori_loop(
             0, steps, score_turn, jnp.full((8, qn), NEGATIVE, jnp.float32)
@@ -276,15 +289,29 @@
         peak = jnp.max(peak, axis=0, keepdims=True)
 
         def expo_turn(t, total):
-            e = jnp.exp2(s_ref[h, chunk_rows(t), :] - peak)
-            s_ref[h, chunk_rows(t), :] = e
-            return total + fold_rows(e)
+            for n in range(pieces):
+                e = jnp.exp2(s_ref[h, piece_rows(t, n), :] - peak)
+                s_ref[h, piece_rows(t, n), :] = e
+                for k in range(0, PIECE, 8):
+                    total = total + e[k : k + 8]
+            return total
 
         total = lax.fori_loop(0, steps, expo_turn, jnp.zeros((8, qn), jnp.float32))
         stat_ref[ka, h : h + 1, :] = peak
         stat_ref[ka, heads + h : heads + h + 1, :] = jnp.sum(
             total, axis=0, keepdims=True
         )
+
+    def stats(first, last):
+        @pl.when(diagonal)
+        def _():
+            for h in range(first, last):
+                head_stats(h, True)
+
+        @pl.when(z > ka)
+        def _():
+            for h in range(first, last):
+                head_stats(h, False)
 
     @pl.when(live)
     def _():
@@ -303,10 +330,7 @@
     loads[0].wait()
     loads[1].wait()
 
-    @pl.when(live)
-    def _():
-        for h in range(heads // 2):
-            head_stats(h)
+    stats(0, heads // 2)
 
     for load in loads[2:]:
         load.wait()
@@ -315,8 +339,7 @@
     @pl.when(live)
     def _():
         pair_copy(core).start()
-        for h in range(heads // 2, heads):
-            head_stats(h)
+        stats(heads // 2, heads)
 
         @pl.loop(1, na)
         def _(k):
@@ -344,7 +367,8 @@
         c_all = c_ref[...]
         for h in range(heads):
             ch_ref[h] = jnp.where(head_of == h, c_all, jnp.zeros_like(c_all))
-        bt_ref[...] = jnp.transpose(b_ref[...])
+        for t in range(steps):
+            bt_ref[t] = jnp.transpose(b_ref[t * CHUNK : (t + 1) * CHUNK, :])
 
         scan_ref[...] = jnp.zeros_like(scan_ref)
         scan_ref[0:heads, :] = pair_ref[core]
@@ -401,50 +425,102 @@
         own_peak = stat_ref[ka, 0:heads, :]
         scaling = jnp.exp2(own_peak - peak) / total
 
-        def grad_turn(t, row_sums):
-            rows = chunk_rows(t)
-            mask = mask_of(t)
-            b_rows = b_ref[rows, :]
-            out = jnp.zeros((CHUNK, cols), jnp.float32)
-            new_sums = []
+        def send_grad_b(t):
+            gx_copy(t * per_chunk, per_chunk).wait_recv()
+
+            @pl.loop(0, per_chunk)
+            def _(k):
+                target = t * per_chunk + k
+                sums = gbpart_ref[target, core] + gbsib_ref[target]
+
+                @pl.when(target == z)
+                def _():
+                    gbown_ref[...] = sums
+
+                @pl.when(target != z)
+                def _():
+                    gbsend_ref[target] = sums.astype(jnp.bfloat16)
+                    gb_copy(z, target).start()
+
+        def turn_chunk(n):
+            return lax.rem(n + z // per_chunk, steps)
+
+        def grad_pass(masked):
+            def grad_turn(n, row_sums):
+                t = turn_chunk(n)
+                rows = chunk_rows(t)
+                b_rows = b_ref[rows, :]
+                inners = [dot(b_rows, ch_ref[h], ((1,), (1,))) for h in range(heads)]
+                out = jnp.zeros((CHUNK, cols), jnp.float32)
+                new_sums = []
+                for h in range(heads):
+                    sums = row_sums[h]
+                    weights = []
+                    folds = []
+                    for m in range(pieces):
+                        at = piece_rows(t, m)
+                        column = kcol_ref[h, at, :]
+                        gap = (
+                            jnp.concatenate([column] * (qn // 128), axis=1)
+                            - arow[h : h + 1, :]
+                        )
+                        if masked:
+                            gap = jnp.where(mask_of(t, m), gap, NEGATIVE)
+                        decay = jnp.exp2(gap)
+                        student = inners[h][m * PIECE : (m + 1) * PIECE] * decay
+                        grad = student - s_ref[h, at, :] * scaling[h : h + 1, :]
+                        weights.append((grad * decay).astype(jnp.bfloat16))
+                        related = grad * student
+                        folds.append(fold_lanes(related))
+                        for k in range(0, PIECE, 8):
+                            sums = sums + related[k : k + 8]
+                    new_sums.append(sums)
+                    weight = jnp.concatenate(weights, axis=0)
+                    out = out + dot(weight, ch_ref[h], ((1,), (0,)))
+                    low = slice(h * state, (h + 1) * state)
+                    turned = bt_ref[t, low, :]
+                    gct_ref[low, :] += dot(turned, weight, ((1,), (0,)))
+                    fold = jnp.concatenate(folds, axis=0)
+                    for k in range(blocks):
+                        flipped = jnp.transpose(fold[k * 128 : (k + 1) * 128])
+                        cs_ref[t * blocks + k, h : h + 1, :] = jnp.sum(
+                            flipped, axis=0, keepdims=True
+                        )
+                gbpart_ref[pl.ds(t * per_chunk, per_chunk)] = (out * factor).reshape(
+                    per_chunk, 2, gb_rows, cols
+                )
+                gx_copy(t * per_chunk, per_chunk).start()
+
+                @pl.when(n > 0)
+                def _():
+                    send_grad_b(turn_chunk(n - 1))
+
+                return tuple(new_sums)
+
+            row_sums = lax.fori_loop(
+                0,
+                steps,
+                grad_turn,
+                tuple(jnp.zeros((8, qn), jnp.float32) for _ in range(heads)),
+            )
             for h in range(heads):
-                inner = dot(b_rows, ch_ref[h], ((1,), (1,)))
-                gap = jnp.concatenate(
-                    [kcol_ref[h, rows, :]] * (qn // 128), axis=1
-                ) - arow[h : h + 1, :]
-                decay = jnp.exp2(jnp.where(mask, gap, NEGATIVE))
-                student = inner * decay
-                grad = student - s_ref[h, rows, :] * scaling[h : h + 1, :]
-                weight = (grad * decay).astype(jnp.bfloat16)
-                w_ref[h, rows, :] = weight
-                related = grad * student
-                flipped = jnp.transpose(fold_lanes(related))
-                cs_ref[t, h : h + 1, :] = jnp.sum(flipped, axis=0, keepdims=True)
-                new_sums.append(row_sums[h] + fold_rows(related))
-                out = out + dot(weight, ch_ref[h], ((1,), (0,)))
-            gbpart_ref[pl.ds(t * per_chunk, per_chunk)] = (out * factor).reshape(
-                per_chunk, 2, gb_rows, cols
-            )
-            gx_copy(t * per_chunk, per_chunk).start()
-            return tuple(new_sums)
-
-        row_sums = lax.fori_loop(
-            0,
-            steps,
-            grad_turn,
-            tuple(jnp.zeros((8, qn), jnp.float32) for _ in range(heads)),
-        )
+                rs_ref[h] = row_sums[h]
+
+        gct_ref[...] = jnp.zeros_like(gct_ref)
+
+        @pl.when(diagonal)
+        def _():
+            grad_pass(True)
+
+        @pl.when(z > ka)
+        def _():
+            grad_pass(False)
+
         cs_copy().start()
 
         for h in range(heads):
-            slope_ref[ka, h : h + 1, 0:qn] = jnp.sum(
-                row_sums[h], axis=0, keepdims=True
-            )
-            flat = dot(
-                bt_ref[h * state : (h + 1) * state, :], w_ref[h], ((1,), (0,))
-            )
-            gcown_ref[:, h * state : (h + 1) * state] = jnp.transpose(flat * factor)
-
+            slope_ref[ka, h : h + 1, 0:qn] = jnp.sum(rs_ref[h], axis=0, keepdims=True)
+        gcown_ref[...] = jnp.transpose(gct_ref[...] * factor)
         gcsend_ref[...] = (
             gcown_ref[...].reshape(na, gc_rows, cols).astype(jnp.bfloat16)
         )
@@ -467,17 +543,7 @@
         def _(k):
             gc_copy(ka, lax.rem(ka + k, na)).start()
 
-        gx_copy(0, nz).wait_recv()
-
-        @pl.loop(1, nz)
-        def _(k):
-            target = lax.rem(z + k, nz)
-            gbsend_ref[target] = (
-                gbpart_ref[target, core] + gbsib_ref[target]
-            ).astype(jnp.bfloat16)
-            gb_copy(z, target).start()
-
-        gbown_ref[...] = gbpart_ref[z, core] + gbsib_ref[z]
+        send_grad_b(turn_chunk(steps - 1))
 
         def later_turn(slot, total):
             fold_copy(slot, z).wait_recv()
@@ -499,7 +565,7 @@
             )
             everything = above + colsend_ref[...]
             for k in range(half):
-                lanes = slice(k * CHUNK, (k + 1) * CHUNK)
+                lanes = slice(k * 128, (k + 1) * 128)
                 slope_ref[ka, :, lanes] = slope_ref[ka, :, lanes] - everything[k]
 
             @pl.when(core == 0)
@@ -539,7 +605,9 @@
     @pl.when(live)
     def _():
         pair_copy(core).wait_send()
-        gx_copy(0, nz).wait_send()
+        to(
+            gbpart_ref.at[pl.ds(0, nz), other], gbsib_ref, gx_send, gx_recv.at[0], (sibling, ka)
+        ).wait_send()
         cs_copy().wait_send()
 
         @pl.when(jnp.logical_not(diagonal))
@@ -592,6 +660,19 @@
     def _():
         rest = pl.ds(0, na - 1)
         to(slope_ref.at[rest], slope_ref.at[rest], slope_send, slope_recv.at[0], (pb, ka)).wait_send()
+
+
+def place(gc_in, gb_in, gr_in, gc_out, gb_out, gr_out, sem):
+    copies = [
+        pltpu.make_async_copy(src, dst, sem.at[n])
+        for n, (src, dst) in enumerate(
+            ((gc_in, gc_out), (gb_in, gb_out), (gr_in, gr_out))
+        )
+    ]
+    for copy in copies:
+        copy.start()
+    for copy in copies:
+        copy.wait()
 
 
 def body(teacher_query, teacher_key, student_c, student_b, decay_rate):
@@ -608,13 +689,14 @@
     hbm = pl.BlockSpec(memory_space=pl.ANY)
     dma = pltpu.SemaphoreType.DMA
     scan_rows = -(-heads * 3 // 8) * 8
-    return pl.pallas_call(
+    shapes = (
+        jax.ShapeDtypeStruct((qn // na, cols), f32),
+        jax.ShapeDtypeStruct((kn // nb, cols), f32),
+        jax.ShapeDtypeStruct((heads, qn), f32),
+    )
+    results = pl.pallas_call(
         functools.partial(kernel, nb, na, heads),
-        out_shape=(
-            jax.ShapeDtypeStruct((qn // na, cols), f32),
-            jax.ShapeDtypeStruct((kn // nb, cols), f32),
-            jax.ShapeDtypeStruct((heads, qn), f32),
-        ),
+        out_shape=shapes,
         in_specs=[hbm, hbm, hbm, hbm, hbm],
         out_specs=[vmem, vmem, vmem],
         scratch_shapes=[
@@ -623,7 +705,7 @@
             pltpu.VMEM((qn, cols), bf16),
             pltpu.VMEM((kn, cols), bf16),
             pltpu.VMEM((heads, qn, cols), bf16),
-            pltpu.VMEM((cols, kn), bf16),
+            pltpu.VMEM((steps, cols, CHUNK), bf16),
             pltpu.VMEM((heads, kn, qn), f32),
             pltpu.VMEM((heads, kn, qn), bf16),
             pltpu.VMEM((heads, kn, 128), f32),
@@ -632,12 +714,14 @@
             pltpu.VMEM((2, heads, qn), f32),
             pltpu.VMEM((nz, 2, heads, 128), f32),
             pltpu.VMEM((na, 2 * heads, qn), f32),
-            pltpu.VMEM((steps, heads, CHUNK), f32),
-            pltpu.VMEM((steps, heads, CHUNK), f32),
-            pltpu.VMEM((nz, heads, CHUNK), f32),
-            pltpu.VMEM((steps // 2, heads, CHUNK), f32),
-            pltpu.VMEM((nz, steps // 2, heads, CHUNK), f32),
+            pltpu.VMEM((kn // 128, heads, 128), f32),
+            pltpu.VMEM((kn // 128, heads, 128), f32),
+            pltpu.VMEM((nz, heads, 128), f32),
+            pltpu.VMEM((qn // 128, heads, 128), f32),
+            pltpu.VMEM((nz, qn // 128, heads, 128), f32),
             pltpu.VMEM((na, heads, qn + 128), f32),
+            pltpu.VMEM((heads, 8, qn), f32),
+            pltpu.VMEM((cols, qn), f32),
             pltpu.VMEM((nz, 2, kn // nb, cols), f32),
             pltpu.VMEM((nz, kn // nb, cols), f32),
             pltpu.VMEM((kn // nb, cols), f32),
@@ -663,7 +747,7 @@
             dma,
             dma((na,)),
             dma,
-            dma,
+            dma((steps,)),
             dma,
             dma((nz,)),
             dma,
@@ -673,6 +757,14 @@
             collective_id=0, has_side_effects=True, vmem_limit_bytes=62 * 1024 * 1024
         ),
     )(teacher_query, teacher_key, student_c, student_b, decay_rate)
+    return pl.pallas_call(
+        place,
+        out_shape=shapes,
+        in_specs=[hbm, hbm, hbm],
+        out_specs=[hbm, hbm, hbm],
+        scratch_shapes=[dma((3,))],
+        compiler_params=pltpu.CompilerParams(vmem_limit_bytes=62 * 1024 * 1024),
+    )(*results)
 
 
 def solution(mesh):

time: 50.2 us -> 48.8 us (0.972)
  the two profiles are of different devices: /device:TPU:1 before, /device:TPU:64 now
where the time goes in v3:
time: 48.8 us; the launch traced here: 48.7 us
  Pallas kernels  48 us (98%)
  between operations  0.64 us (1%)
    pallas_call x1, Pallas kernels, body(): pl.pallas_call(functools.partial(kernel, nb, na, heads), out_shape=shapes...  45.8 us
    pallas_call x1, Pallas kernels, body(): pl.pallas_call(place, out_shape=shapes, in_specs=[hbm, hbm, hbm], out_spe...  2.25 us

profile of v3, /device:TPU:64, one launch (start us, length us, event | category | flops | bytes accessed | tf_op | source)
XLA Modules:
  0.0 48.7 jit_solution(7909866377471466020)
XLA Ops:
  0.6 45.8 %shard_map.76 = (f32[32,128]{1,0:T(8,128)}, f32[32,128]{1,0:T(8,128)}, f32[2,512]{1,0:T(2,128)}) custom-call(bf16[512,256]{1,0:T(8,128)(2,1)} %q_hbm.1, bf16[1024,256]{1,0:T(8,128)(2,1)} %k_hbm.1, bf16[512,128]{1,0:T(8,128)(2,1)} %c_hbm.1, bf16[1024,128]{1,0:T(8,128)(2,1)} %b_hbm.1, f32[2,512]{1,0:T(2,128)} %rate_hbm.1), custom_call_target="tpu_custom_call" | custom-call | tf_op jit(solution)/shard_map/pallas_call | solution.py:697
  46.4 2.2 %shard_map.77 = (f32[32,128]{1,0:T(8,128)}, f32[32,128]{1,0:T(8,128)}, f32[2,512]{1,0:T(2,128)}) custom-call(f32[32,128]{1,0:T(8,128)} %get-tuple-element.6.gc_in, f32[32,128]{1,0:T(8,128)} %get-tuple-element.7.gb_in, f32[2,512]{1,0:T(2,128)} %get-tuple-element.8.gr_in), custom_call_target="tpu_custom_call" | custom-call | tf_op jit(solution)/shard_map/pallas_call | solution.py:760

commit v4 on v3

--- a/solution.py
+++ b/solution.py
@@ -60,6 +60,8 @@
     ch_ref,
     bt_ref,
     s_ref,
+    st_ref,
+    dec_ref,
     w_ref,
     kcol_ref,
     scan_ref,
@@ -74,7 +76,6 @@
     col_ref,
     slope_ref,
     rs_ref,
-    gct_ref,
     gbpart_ref,
     gbsib_ref,
     gbown_ref,
@@ -341,14 +342,6 @@
         pair_copy(core).start()
         stats(heads // 2, heads)
 
-        @pl.loop(1, na)
-        def _(k):
-            target = lax.rem(ka + k, na)
-
-            @pl.when(target <= z)
-            def _():
-                stat_copy(ka, target).start()
-
         pair_copy(other).wait_recv()
         own_fold = jnp.stack([fold_lanes(pair_ref[0]), fold_lanes(pair_ref[1])])
         rfold_ref[z] = own_fold
@@ -363,12 +356,19 @@
             def _():
                 rfold_copy(z, target).start()
 
+        @pl.loop(1, na)
+        def _(k):
+            target = lax.rem(ka + k, na)
+
+            @pl.when(target <= z)
+            def _():
+                stat_copy(ka, target).start()
+
         head_of = lax.broadcasted_iota(jnp.int32, (qn, cols), 1) // state
         c_all = c_ref[...]
         for h in range(heads):
             ch_ref[h] = jnp.where(head_of == h, c_all, jnp.zeros_like(c_all))
-        for t in range(steps):
-            bt_ref[t] = jnp.transpose(b_ref[t * CHUNK : (t + 1) * CHUNK, :])
+        bt_ref[...] = jnp.transpose(b_ref[...])
 
         scan_ref[...] = jnp.zeros_like(scan_ref)
         scan_ref[0:heads, :] = pair_ref[core]
@@ -412,51 +412,13 @@
         )
         arow = (scan_ref[0:heads, :] + before) * LOG2E
 
-        @pl.loop(0, z + 1)
-        def _(slot):
-            @pl.when(slot != ka)
-            def _():
-                stat_copy(slot, slot).wait_recv()
-
-        peaks = stat_ref[:, 0:heads, :]
-        totals = stat_ref[:, heads : 2 * heads, :]
-        peak = jnp.max(peaks, axis=0)
-        total = jnp.sum(totals * jnp.exp2(peaks - peak[None]), axis=0)
-        own_peak = stat_ref[ka, 0:heads, :]
-        scaling = jnp.exp2(own_peak - peak) / total
-
-        def send_grad_b(t):
-            gx_copy(t * per_chunk, per_chunk).wait_recv()
-
-            @pl.loop(0, per_chunk)
-            def _(k):
-                target = t * per_chunk + k
-                sums = gbpart_ref[target, core] + gbsib_ref[target]
-
-                @pl.when(target == z)
-                def _():
-                    gbown_ref[...] = sums
-
-                @pl.when(target != z)
-                def _():
-                    gbsend_ref[target] = sums.astype(jnp.bfloat16)
-                    gb_copy(z, target).start()
-
-        def turn_chunk(n):
-            return lax.rem(n + z // per_chunk, steps)
-
-        def grad_pass(masked):
-            def grad_turn(n, row_sums):
-                t = turn_chunk(n)
-                rows = chunk_rows(t)
-                b_rows = b_ref[rows, :]
+        def student_pass(masked):
+            def student_turn(t, sums):
+                b_rows = b_ref[chunk_rows(t), :]
                 inners = [dot(b_rows, ch_ref[h], ((1,), (1,))) for h in range(heads)]
-                out = jnp.zeros((CHUNK, cols), jnp.float32)
                 new_sums = []
                 for h in range(heads):
-                    sums = row_sums[h]
-                    weights = []
-                    folds = []
+                    squares, mixed = sums[h]
                     for m in range(pieces):
                         at = piece_rows(t, m)
                         column = kcol_ref[h, at, :]
@@ -468,59 +430,99 @@
                             gap = jnp.where(mask_of(t, m), gap, NEGATIVE)
                         decay = jnp.exp2(gap)
                         student = inners[h][m * PIECE : (m + 1) * PIECE] * decay
-                        grad = student - s_ref[h, at, :] * scaling[h : h + 1, :]
-                        weights.append((grad * decay).astype(jnp.bfloat16))
-                        related = grad * student
-                        folds.append(fold_lanes(related))
+                        dec_ref[h, at, :] = decay
+                        st_ref[h, at, :] = student
+                        square = student * student
+                        mix = student * s_ref[h, at, :]
                         for k in range(0, PIECE, 8):
-                            sums = sums + related[k : k + 8]
-                    new_sums.append(sums)
-                    weight = jnp.concatenate(weights, axis=0)
-                    out = out + dot(weight, ch_ref[h], ((1,), (0,)))
-                    low = slice(h * state, (h + 1) * state)
-                    turned = bt_ref[t, low, :]
-                    gct_ref[low, :] += dot(turned, weight, ((1,), (0,)))
-                    fold = jnp.concatenate(folds, axis=0)
-                    for k in range(blocks):
-                        flipped = jnp.transpose(fold[k * 128 : (k + 1) * 128])
-                        cs_ref[t * blocks + k, h : h + 1, :] = jnp.sum(
-                            flipped, axis=0, keepdims=True
-                        )
-                gbpart_ref[pl.ds(t * per_chunk, per_chunk)] = (out * factor).reshape(
-                    per_chunk, 2, gb_rows, cols
-                )
-                gx_copy(t * per_chunk, per_chunk).start()
-
-                @pl.when(n > 0)
-                def _():
-                    send_grad_b(turn_chunk(n - 1))
-
+                            squares = squares + square[k : k + 8]
+                            mixed = mixed + mix[k : k + 8]
+                    new_sums.append((squares, mixed))
                 return tuple(new_sums)
 
-            row_sums = lax.fori_loop(
-                0,
-                steps,
-                grad_turn,
-                tuple(jnp.zeros((8, qn), jnp.float32) for _ in range(heads)),
+            zero = jnp.zeros((8, qn), jnp.float32)
+            sums = lax.fori_loop(
+                0, steps, student_turn, tuple((zero, zero) for _ in range(heads))
             )
             for h in range(heads):
-                rs_ref[h] = row_sums[h]
-
-        gct_ref[...] = jnp.zeros_like(gct_ref)
+                rs_ref[h, 0] = sums[h][0]
+                rs_ref[h, 1] = sums[h][1]
 
         @pl.when(diagonal)
         def _():
-            grad_pass(True)
+            student_pass(True)
 
         @pl.when(z > ka)
         def _():
-            grad_pass(False)
-
+            student_pass(False)
+
+        @pl.loop(0, z + 1)
+        def _(slot):
+            @pl.when(slot != ka)
+            def _():
+                stat_copy(slot, slot).wait_recv()
+
+        peaks = stat_ref[:, 0:heads, :]
+        totals = stat_ref[:, heads : 2 * heads, :]
+        peak = jnp.max(peaks, axis=0)
+        total = jnp.sum(totals * jnp.exp2(peaks - peak[None]), axis=0)
+        own_peak = stat_ref[ka, 0:heads, :]
+        scaling = jnp.exp2(own_peak - peak) / total
+
+        def send_grad_b(t):
+            gx_copy(t * per_chunk, per_chunk).wait_recv()
+
+            @pl.loop(0, per_chunk)
+            def _(k):
+                target = t * per_chunk + k
+                sums = gbpart_ref[target, core] + gbsib_ref[target]
+
+                @pl.when(target == z)
+                def _():
+                    gbown_ref[...] = sums
+
+                @pl.when(target != z)
+                def _():
+                    gbsend_ref[target] = sums.astype(jnp.bfloat16)
+                    gb_copy(z, target).start()
+
+        def weight_turn(t, carry):
+            out = jnp.zeros((CHUNK, cols), jnp.float32)
+            for h in range(heads):
+                weights = []
+                folds = []
+                for m in range(pieces):
+                    at = piece_rows(t, m)
+                    student = st_ref[h, at, :]
+                    grad = student - s_ref[h, at, :] * scaling[h : h + 1, :]
+                    weights.append((grad * dec_ref[h, at, :]).astype(jnp.bfloat16))
+                    folds.append(fold_lanes(grad * student))
+                weight = jnp.concatenate(weights, axis=0)
+                w_ref[h, chunk_rows(t), :] = weight
+                out = out + dot(weight, ch_ref[h], ((1,), (0,)))
+                fold = jnp.concatenate(folds, axis=0)
+                for k in range(blocks):
+                    flipped = jnp.transpose(fold[k * 128 : (k + 1) * 128])
+                    cs_ref[t * blocks + k, h : h + 1, :] = jnp.sum(
+                        flipped, axis=0, keepdims=True
+                    )
+            gbpart_ref[pl.ds(t * per_chunk, per_chunk)] = (out * factor).reshape(
+                per_chunk, 2, gb_rows, cols
+            )
+            gx_copy(t * per_chunk, per_chunk).start()
+            return carry
+
+        lax.fori_loop(0, steps, weight_turn, 0)
         cs_copy().start()
 
         for h in range(heads):
-            slope_ref[ka, h : h + 1, 0:qn] = jnp.sum(rs_ref[h], axis=0, keepdims=True)
-        gcown_ref[...] = jnp.transpose(gct_ref[...] * factor)
+            slope_ref[ka, h : h + 1, 0:qn] = jnp.sum(
+                rs_ref[h, 0], axis=0, keepdims=True
+            ) - scaling[h : h + 1, :] * jnp.sum(rs_ref[h, 1], axis=0, keepdims=True)
+            flat = dot(
+                bt_ref[h * state : (h + 1) * state, :], w_ref[h], ((1,), (0,))
+            )
+            gcown_ref[:, h * state : (h + 1) * state] = jnp.transpose(flat * factor)
         gcsend_ref[...] = (
             gcown_ref[...].reshape(na, gc_rows, cols).astype(jnp.bfloat16)
         )
@@ -539,11 +541,13 @@
         def _(target):
             fold_copy(z, target).start()
 
+        @pl.loop(0, steps)
+        def _(n):
+            send_grad_b(lax.rem(n + z // per_chunk, steps))
+
         @pl.loop(1, na)
         def _(k):
             gc_copy(ka, lax.rem(ka + k, na)).start()
-
-        send_grad_b(turn_chunk(steps - 1))
 
         def later_turn(slot, total):
             fold_copy(slot, z).wait_recv()
@@ -696,7 +700,7 @@
     )
     results = pl.pallas_call(
         functools.partial(kernel, nb, na, heads),
-        out_shape=shapes,
+        out_shape=tuple(pltpu.VMEM(shape.shape, f32) for shape in shapes),
         in_specs=[hbm, hbm, hbm, hbm, hbm],
         out_specs=[vmem, vmem, vmem],
         scratch_shapes=[
@@ -705,7 +709,9 @@
             pltpu.VMEM((qn, cols), bf16),
             pltpu.VMEM((kn, cols), bf16),
             pltpu.VMEM((heads, qn, cols), bf16),
-            pltpu.VMEM((steps, cols, CHUNK), bf16),
+            pltpu.VMEM((cols, kn), bf16),
+            pltpu.VMEM((heads, kn, qn), f32),
+            pltpu.VMEM((heads, kn, qn), f32),
             pltpu.VMEM((heads, kn, qn), f32),
             pltpu.VMEM((heads, kn, qn), bf16),
             pltpu.VMEM((heads, kn, 128), f32),
@@ -720,8 +726,7 @@
             pltpu.VMEM((qn // 128, heads, 128), f32),
             pltpu.VMEM((nz, qn // 128, heads, 128), f32),
             pltpu.VMEM((na, heads, qn + 128), f32),
-            pltpu.VMEM((heads, 8, qn), f32),
-            pltpu.VMEM((cols, qn), f32),
+            pltpu.VMEM((heads, 2, 8, qn), f32),
             pltpu.VMEM((nz, 2, kn // nb, cols), f32),
             pltpu.VMEM((nz, kn // nb, cols), f32),
             pltpu.VMEM((kn // nb, cols), f32),
@@ -754,16 +759,15 @@
             dma((na,)),
         ],
         compiler_params=pltpu.CompilerParams(
-            collective_id=0, has_side_effects=True, vmem_limit_bytes=62 * 1024 * 1024
+            collective_id=0, has_side_effects=True, vmem_limit_bytes=60 * 1024 * 1024
         ),
     )(teacher_query, teacher_key, student_c, student_b, decay_rate)
     return pl.pallas_call(
         place,
         out_shape=shapes,
-        in_specs=[hbm, hbm, hbm],
+        in_specs=[vmem, vmem, vmem],
         out_specs=[hbm, hbm, hbm],
         scratch_shapes=[dma((3,))],
-        compiler_params=pltpu.CompilerParams(vmem_limit_bytes=62 * 1024 * 1024),
     )(*results)
 
 

time: 48.8 us -> 49.4 us (1.012)
  the two profiles are of different devices: /device:TPU:64 before, /device:TPU:1 now
where the time goes in v4:
time: 49.4 us; the launch traced here: 49.2 us
  Pallas kernels  46.8 us (95%)
  local copies, waits for them, and re-layouts  1.78 us (4%)
  between operations  0.65 us (1%)
    pallas_call x1, Pallas kernels, body(): pl.pallas_call(functools.partial(kernel, nb, na, heads), out_shape=tuple(...  45.4 us
    unnamed x6, local copies, waits for them, and re-layouts  1.78 us
    pallas_call x1, Pallas kernels, body(): pl.pallas_call(place, out_shape=shapes, in_specs=[vmem, vmem, vmem], out_...  1.37 us

profile of v4, /device:TPU:1, one launch (start us, length us, event | category | flops | bytes accessed | tf_op | source)
XLA Modules:
  0.0 49.2 jit_solution(7397100818919803153)
XLA Ops:
  0.6 45.4 %shard_map.76 = (f32[32,128]{1,0:T(8,128)S(1)}, f32[32,128]{1,0:T(8,128)S(1)}, f32[2,512]{1,0:T(2,128)S(1)}) custom-call(bf16[512,256]{1,0:T(8,128)(2,1)} %q_hbm.1, bf16[1024,256]{1,0:T(8,128)(2,1)} %k_hbm.1, bf16[512,128]{1,0:T(8,128)(2,1)} %c_hbm.1, bf16[1024,128]{1,0:T(8,128)(2,1)} %b_hbm.1, f32[2,512]{1,0:T(2,128)} %rate_hbm.1), custom_call_target="tpu_custom_call" | custom-call | tf_op jit(solution)/shard_map/pallas_call | solution.py:701
  46.0 0.0 copy-start
  46.0 0.6 %copy-done = f32[32,128]{1,0:T(8,128)} copy-done((f32[32,128]{1,0:T(8,128)}, f32[32,128]{1,0:T(8,128)S(1)}, u32[]{:S(2)}) %copy-start) | copy-done | bytes 16408
  46.6 0.0 copy-start.1
  46.6 0.6 %copy-done.1 = f32[32,128]{1,0:T(8,128)} copy-done((f32[32,128]{1,0:T(8,128)}, f32[32,128]{1,0:T(8,128)S(1)}, u32[]{:S(2)}) %copy-start.1) | copy-done | bytes 16408
  47.2 0.0 copy-start.2
  47.2 0.6 %copy-done.2 = f32[2,512]{1,0:T(2,128)} copy-done((f32[2,512]{1,0:T(2,128)}, f32[2,512]{1,0:T(2,128)S(1)}, u32[]{:S(2)}) %copy-start.2) | copy-done | bytes 4120
  47.8 1.4 %shard_map.77 = (f32[32,128]{1,0:T(8,128)}, f32[32,128]{1,0:T(8,128)}, f32[2,512]{1,0:T(2,128)}) custom-call(f32[32,128]{1,0:T(8,128)} %copy-done, f32[32,128]{1,0:T(8,128)} %copy-done.1, f32[2,512]{1,0:T(2,128)} %copy-done.2), custom_call_target="tpu_custom_call" | custom-call | tf_op jit(solution)/shard_map/pallas_call | solution.py:765
Async XLA Ops:
  46.0 0.6 %copy-start = (f32[32,128]{1,0:T(8,128)}, f32[32,128]{1,0:T(8,128)S(1)}, u32[]{:S(2)}) copy-start(f32[32,128]{1,0:T(8,128)S(1)} %get-tuple-element.6.gc_in) | copy-start | bytes 49156
  46.6 0.6 %copy-start.1 = (f32[32,128]{1,0:T(8,128)}, f32[32,128]{1,0:T(8,128)S(1)}, u32[]{:S(2)}) copy-start(f32[32,128]{1,0:T(8,128)S(1)} %get-tuple-element.7.gb_in) | copy-start | bytes 49156
  47.2 0.6 %copy-start.2 = (f32[2,512]{1,0:T(2,128)}, f32[2,512]{1,0:T(2,128)S(1)}, u32[]{:S(2)}) copy-start(f32[2,512]{1,0:T(2,128)S(1)} %get-tuple-element.8.gr_in) | copy-start | bytes 12292

commit v5 on v4

--- a/solution.py
+++ b/solution.py
@@ -65,14 +65,12 @@
     w_ref,
     kcol_ref,
     scan_ref,
-    pair_ref,
+    rate_ref,
     krate_ref,
     rfold_ref,
     stat_ref,
     cs_ref,
-    cssib_ref,
     fold_ref,
-    colsend_ref,
     col_ref,
     slope_ref,
     rs_ref,
@@ -85,15 +83,11 @@
     gcsend_ref,
     gcrecv_ref,
     in_sem,
-    pair_send,
-    pair_recv,
     rate_send,
     krate_recv,
     rfold_recv,
     stat_send,
     stat_recv,
-    cs_send,
-    cs_recv,
     fold_send,
     fold_recv,
     col_send,
@@ -127,6 +121,7 @@
     gc_rows = qn // na
     per_chunk = CHUNK // (2 * gb_rows)
     factor = 2.0 * qn * nb
+    first = 2 * ka
     live = z >= ka
     diagonal = z == ka
 
@@ -136,7 +131,7 @@
             (
                 (q_hbm, q_ref),
                 (k_hbm, k_ref),
-                (rate_hbm, pair_ref.at[core]),
+                (rate_hbm, rate_ref),
                 (c_hbm, c_ref),
                 (b_hbm, b_ref),
             )
@@ -146,7 +141,6 @@
         load.start()
 
     barrier = pltpu.get_barrier_semaphore()
-    pl.semaphore_signal(barrier, inc=1, device_id=(sibling, ka), device_id_type=MESH)
 
     @pl.loop(1, na)
     def _(k):
@@ -154,13 +148,10 @@
             barrier, inc=1, device_id=(pb, lax.rem(ka + k, na)), device_id_type=MESH
         )
 
-    @pl.loop(1, nz)
+    @pl.loop(1, nb)
     def _(k):
         pl.semaphore_signal(
-            barrier,
-            inc=1,
-            device_id=(2 * lax.rem(z + k, nz) + core, ka),
-            device_id_type=MESH,
+            barrier, inc=1, device_id=(lax.rem(pb + k, nb), ka), device_id_type=MESH
         )
 
     def to(src, dst, send, recv, device):
@@ -176,13 +167,14 @@
     def up(target):
         return (2 * target + core, ka)
 
-    def pair_copy(slot):
-        return to(
-            pair_ref.at[slot], pair_ref.at[slot], pair_send, pair_recv, (sibling, ka)
-        )
-
-    def krate_copy(target):
-        return to(pair_ref, krate_ref, rate_send.at[target], krate_recv, up(target))
+    def krate_copy(slot, target):
+        return to(
+            rate_ref,
+            krate_ref.at[slot],
+            rate_send.at[target],
+            krate_recv.at[slot],
+            (target, ka),
+        )
 
     def rfold_copy(slot, target):
         return to(
@@ -190,7 +182,7 @@
             rfold_ref.at[slot],
             rate_send.at[target],
             rfold_recv.at[slot],
-            up(target),
+            (target, ka),
         )
 
     def stat_copy(slot, target):
@@ -202,21 +194,22 @@
             (pb, target),
         )
 
-    def cs_copy():
-        return to(cs_ref, cssib_ref, cs_send, cs_recv, (sibling, ka))
-
     def fold_copy(slot, target):
         return to(
             fold_ref.at[slot],
             fold_ref.at[slot],
             fold_send.at[target],
             fold_recv.at[slot],
-            up(target),
-        )
-
-    def col_copy(slot):
-        return to(
-            colsend_ref, col_ref.at[slot], col_send, col_recv.at[slot], up(ka)
+            (target, ka),
+        )
+
+    def col_copy(part, slot):
+        return to(
+            cs_ref.at[pl.ds(part * half, half)],
+            col_ref.at[slot],
+            col_send.at[part],
+            col_recv.at[slot],
+            (first + part, ka),
         )
 
     def slope_copy(slot, target):
@@ -331,30 +324,25 @@
     loads[0].wait()
     loads[1].wait()
 
-    stats(0, heads // 2)
+    stats(0, heads)
 
     for load in loads[2:]:
         load.wait()
-    pl.semaphore_wait(barrier, na + nz - 1)
+    pl.semaphore_wait(barrier, na + nb - 2)
 
     @pl.when(live)
     def _():
-        pair_copy(core).start()
-        stats(heads // 2, heads)
-
-        pair_copy(other).wait_recv()
-        own_fold = jnp.stack([fold_lanes(pair_ref[0]), fold_lanes(pair_ref[1])])
-        rfold_ref[z] = own_fold
-
-        @pl.loop(z + 1, nz)
+        rfold_ref[pb] = fold_lanes(rate_ref[...])
+
+        @pl.loop(pb + 1, nb)
         def _(target):
             @pl.when(diagonal)
             def _():
-                krate_copy(target).start()
+                krate_copy(core, target).start()
 
             @pl.when(jnp.logical_not(diagonal))
             def _():
-                rfold_copy(z, target).start()
+                rfold_copy(pb, target).start()
 
         @pl.loop(1, na)
         def _(k):
@@ -370,21 +358,27 @@
             ch_ref[h] = jnp.where(head_of == h, c_all, jnp.zeros_like(c_all))
         bt_ref[...] = jnp.transpose(b_ref[...])
 
-        scan_ref[...] = jnp.zeros_like(scan_ref)
-        scan_ref[0:heads, :] = pair_ref[core]
-
         @pl.when(diagonal)
         def _():
-            for part in range(2):
-                low = heads * (1 + part)
-                scan_ref[low : low + heads, :] = pair_ref[part]
-
-        @pl.when(jnp.logical_not(diagonal))
+            krate_ref[core] = rate_ref[...]
+
+            @pl.when(core == 0)
+            def _():
+                krate_ref[1] = jnp.zeros_like(rate_ref)
+
+        @pl.when(pb > first)
         def _():
-            krate_copy(z).wait_recv()
-            for part in range(2):
-                low = heads * (1 + part)
-                scan_ref[low : low + heads, :] = krate_ref[part]
+            krate_copy(0, pb).wait_recv()
+
+        @pl.when(z > ka)
+        def _():
+            krate_copy(1, pb).wait_recv()
+
+        scan_ref[...] = jnp.zeros_like(scan_ref)
+        scan_ref[0:heads, :] = rate_ref[...]
+        for part in range(2):
+            low = heads * (1 + part)
+            scan_ref[low : low + heads, :] = krate_ref[part]
 
         rates = scan_ref[...]
         scan_ref[...] = lane_prefix(rates)
@@ -400,15 +394,16 @@
                 shift = shift + ends[row : row + 1, :]
 
         def between_turn(slot, total):
-            rfold_copy(slot, z).wait_recv()
-            return total + rfold_ref[slot, 0] + rfold_ref[slot, 1]
+            rfold_copy(slot, pb).wait_recv()
+            return total + rfold_ref[slot]
 
         between = lax.fori_loop(
-            ka + 1, z, between_turn, jnp.zeros((heads, 128), jnp.float32)
-        )
-        between = between + jnp.where(core == 1, rfold_ref[z, 0], 0.0)
-        before = jnp.sum(between, axis=1, keepdims=True) + jnp.where(
-            diagonal, 0.0, ends[heads : 2 * heads] + ends[2 * heads : 3 * heads]
+            first + 2, pb, between_turn, jnp.zeros((heads, 128), jnp.float32)
+        )
+        before = (
+            jnp.sum(between, axis=1, keepdims=True)
+            + jnp.where(pb > first, ends[heads : 2 * heads], 0.0)
+            + jnp.where(z > ka, ends[2 * heads : 3 * heads], 0.0)
         )
         arow = (scan_ref[0:heads, :] + before) * LOG2E
 
@@ -486,26 +481,47 @@
                     gbsend_ref[target] = sums.astype(jnp.bfloat16)
                     gb_copy(z, target).start()
 
-        def weight_turn(t, carry):
-            out = jnp.zeros((CHUNK, cols), jnp.float32)
+        def column_turn(t, carry):
             for h in range(heads):
-                weights = []
                 folds = []
                 for m in range(pieces):
                     at = piece_rows(t, m)
                     student = st_ref[h, at, :]
                     grad = student - s_ref[h, at, :] * scaling[h : h + 1, :]
-                    weights.append((grad * dec_ref[h, at, :]).astype(jnp.bfloat16))
                     folds.append(fold_lanes(grad * student))
-                weight = jnp.concatenate(weights, axis=0)
-                w_ref[h, chunk_rows(t), :] = weight
-                out = out + dot(weight, ch_ref[h], ((1,), (0,)))
                 fold = jnp.concatenate(folds, axis=0)
                 for k in range(blocks):
                     flipped = jnp.transpose(fold[k * 128 : (k + 1) * 128])
                     cs_ref[t * blocks + k, h : h + 1, :] = jnp.sum(
                         flipped, axis=0, keepdims=True
                     )
+            return carry
+
+        lax.fori_loop(0, steps, column_turn, 0)
+        fold_ref[pb] = jnp.sum(cs_ref[...], axis=0)
+
+        for part in range(2):
+
+            @pl.when(pb != first + part)
+            def _(part=part):
+                col_copy(part, pb).start()
+
+        @pl.loop(first, pb)
+        def _(target):
+            fold_copy(pb, target).start()
+
+        def weight_turn(t, carry):
+            out = jnp.zeros((CHUNK, cols), jnp.float32)
+            for h in range(heads):
+                weights = []
+                for m in range(pieces):
+                    at = piece_rows(t, m)
+                    student = st_ref[h, at, :]
+                    grad = student - s_ref[h, at, :] * scaling[h : h + 1, :]
+                    weights.append((grad * dec_ref[h, at, :]).astype(jnp.bfloat16))
+                weight = jnp.concatenate(weights, axis=0)
+                w_ref[h, chunk_rows(t), :] = weight
+                out = out + dot(weight, ch_ref[h], ((1,), (0,)))
             gbpart_ref[pl.ds(t * per_chunk, per_chunk)] = (out * factor).reshape(
                 per_chunk, 2, gb_rows, cols
             )
@@ -513,7 +529,6 @@
             return carry
 
         lax.fori_loop(0, steps, weight_turn, 0)
-        cs_copy().start()
 
         for h in range(heads):
             slope_ref[ka, h : h + 1, 0:qn] = jnp.sum(
@@ -527,20 +542,6 @@
             gcown_ref[...].reshape(na, gc_rows, cols).astype(jnp.bfloat16)
         )
 
-        cs_copy().wait_recv()
-        sib_fold = jnp.sum(cssib_ref[...], axis=0)
-        fold_ref[z] = jnp.sum(cs_ref[...], axis=0) + sib_fold
-        mine = pl.ds(core * half, half)
-        colsend_ref[...] = cs_ref[mine] + cssib_ref[mine]
-
-        @pl.when(jnp.logical_not(diagonal))
-        def _():
-            col_copy(z).start()
-
-        @pl.loop(ka, z)
-        def _(target):
-            fold_copy(z, target).start()
-
         @pl.loop(0, steps)
         def _(n):
             send_grad_b(lax.rem(n + z // per_chunk, steps))
@@ -550,31 +551,31 @@
             gc_copy(ka, lax.rem(ka + k, na)).start()
 
         def later_turn(slot, total):
-            fold_copy(slot, z).wait_recv()
+            fold_copy(slot, pb).wait_recv()
             return total + fold_ref[slot]
 
-        later = lax.fori_loop(
-            z + 1, nz, later_turn, jnp.where(core == 0, sib_fold, 0.0)
-        )
-        slope_ref[ka, :, qn:] = later
+        slope_ref[ka, :, qn:] = lax.fori_loop(
+            pb + 1, nb, later_turn, jnp.zeros((heads, 128), jnp.float32)
+        )
 
         @pl.when(diagonal)
         def _():
             def col_turn(slot, total):
-                col_copy(slot).wait_recv()
+                col_copy(0, slot).wait_recv()
                 return total + col_ref[slot]
 
-            above = lax.fori_loop(
-                z + 1, nz, col_turn, jnp.zeros(colsend_ref.shape, jnp.float32)
+            others = lax.fori_loop(
+                first, pb, col_turn, jnp.zeros(col_ref.shape[1:], jnp.float32)
             )
-            everything = above + colsend_ref[...]
+            others = lax.fori_loop(pb + 1, nb, col_turn, others)
+            everything = others + cs_ref[pl.ds(core * half, half)]
             for k in range(half):
                 lanes = slice(k * 128, (k + 1) * 128)
                 slope_ref[ka, :, lanes] = slope_ref[ka, :, lanes] - everything[k]
 
             @pl.when(core == 0)
             def _():
-                slope_ref[ka, :, qn:] = jnp.sum(above + cssib_ref[mine], axis=0)
+                slope_ref[ka, :, qn:] = jnp.sum(others, axis=0)
 
         @pl.loop(1, na)
         def _(k):
@@ -608,29 +609,29 @@
 
     @pl.when(live)
     def _():
-        pair_copy(core).wait_send()
         to(
             gbpart_ref.at[pl.ds(0, nz), other], gbsib_ref, gx_send, gx_recv.at[0], (sibling, ka)
         ).wait_send()
-        cs_copy().wait_send()
-
-        @pl.when(jnp.logical_not(diagonal))
-        def _():
-            col_copy(z).wait_send()
-
-        @pl.loop(z + 1, nz)
+
+        for part in range(2):
+
+            @pl.when(pb != first + part)
+            def _(part=part):
+                col_copy(part, pb).wait_send()
+
+        @pl.loop(pb + 1, nb)
         def _(target):
             @pl.when(diagonal)
             def _():
-                krate_copy(target).wait_send()
+                krate_copy(core, target).wait_send()
 
             @pl.when(jnp.logical_not(diagonal))
             def _():
-                rfold_copy(z, target).wait_send()
-
-        @pl.loop(ka, z)
+                rfold_copy(pb, target).wait_send()
+
+        @pl.loop(first, pb)
         def _(target):
-            fold_copy(z, target).wait_send()
+            fold_copy(pb, target).wait_send()
 
         @pl.loop(0, z + 1)
         def _(target):
@@ -666,17 +667,23 @@
         to(slope_ref.at[rest], slope_ref.at[rest], slope_send, slope_recv.at[0], (pb, ka)).wait_send()
 
 
-def place(gc_in, gb_in, gr_in, gc_out, gb_out, gr_out, sem):
-    copies = [
-        pltpu.make_async_copy(src, dst, sem.at[n])
-        for n, (src, dst) in enumerate(
-            ((gc_in, gc_out), (gb_in, gb_out), (gr_in, gr_out))
-        )
+def place(gc_in, gb_in, gr_in, gc_out, gb_out, gr_out, gc, gb, gr, sem):
+    triples = ((gc_in, gc, gc_out), (gb_in, gb, gb_out), (gr_in, gr, gr_out))
+    loads = [
+        pltpu.make_async_copy(src, held, sem.at[n])
+        for n, (src, held, _) in enumerate(triples)
     ]
-    for copy in copies:
-        copy.start()
-    for copy in copies:
-        copy.wait()
+    stores = [
+        pltpu.make_async_copy(held, dst, sem.at[n])
+        for n, (_, held, dst) in enumerate(triples)
+    ]
+    for load in loads:
+        load.start()
+    for load, store in zip(loads, stores):
+        load.wait()
+        store.start()
+    for store in stores:
+        store.wait()
 
 
 def body(teacher_query, teacher_key, student_c, student_b, decay_rate):
@@ -700,7 +707,7 @@
     )
     results = pl.pallas_call(
         functools.partial(kernel, nb, na, heads),
-        out_shape=tuple(pltpu.VMEM(shape.shape, f32) for shape in shapes),
+        out_shape=shapes,
         in_specs=[hbm, hbm, hbm, hbm, hbm],
         out_specs=[vmem, vmem, vmem],
         scratch_shapes=[
@@ -716,15 +723,13 @@
             pltpu.VMEM((heads, kn, qn), bf16),
             pltpu.VMEM((heads, kn, 128), f32),
             pltpu.VMEM((scan_rows, qn), f32),
+            pltpu.VMEM((heads, qn), f32),
             pltpu.VMEM((2, heads, qn), f32),
-            pltpu.VMEM((2, heads, qn), f32),
-            pltpu.VMEM((nz, 2, heads, 128), f32),
+            pltpu.VMEM((nb, heads, 128), f32),
             pltpu.VMEM((na, 2 * heads, qn), f32),
             pltpu.VMEM((kn // 128, heads, 128), f32),
-            pltpu.VMEM((kn // 128, heads, 128), f32),
-            pltpu.VMEM((nz, heads, 128), f32),
-            pltpu.VMEM((qn // 128, heads, 128), f32),
-            pltpu.VMEM((nz, qn // 128, heads, 128), f32),
+            pltpu.VMEM((nb, heads, 128), f32),
+            pltpu.VMEM((nb, qn // 128, heads, 128), f32),
             pltpu.VMEM((na, heads, qn + 128), f32),
             pltpu.VMEM((heads, 2, 8, qn), f32),
             pltpu.VMEM((nz, 2, kn // nb, cols), f32),
@@ -736,19 +741,15 @@
             pltpu.VMEM((na, qn // na, cols), bf16),
             pltpu.VMEM((na, qn // na, cols), bf16),
             dma((5,)),
-            dma,
-            dma,
-            dma((nz,)),
-            dma,
-            dma((nz,)),
+            dma((nb,)),
+            dma((2,)),
+            dma((nb,)),
             dma((na,)),
             dma((na,)),
-            dma,
-            dma,
-            dma((nz,)),
-            dma((nz,)),
-            dma,
-            dma((nz,)),
+            dma((nb,)),
+            dma((nb,)),
+            dma((2,)),
+            dma((nb,)),
             dma,
             dma((na,)),
             dma,
@@ -759,15 +760,16 @@
             dma((na,)),
         ],
         compiler_params=pltpu.CompilerParams(
-            collective_id=0, has_side_effects=True, vmem_limit_bytes=60 * 1024 * 1024
+            collective_id=0, has_side_effects=True, vmem_limit_bytes=62 * 1024 * 1024
         ),
     )(teacher_query, teacher_key, student_c, student_b, decay_rate)
     return pl.pallas_call(
         place,
         out_shape=shapes,
-        in_specs=[vmem, vmem, vmem],
+        in_specs=[hbm, hbm, hbm],
         out_specs=[hbm, hbm, hbm],
-        scratch_shapes=[dma((3,))],
+        scratch_shapes=[pltpu.VMEM(shape.shape, f32) for shape in shapes] + [dma((3,))],
+        compiler_params=pltpu.CompilerParams(vmem_limit_bytes=62 * 1024 * 1024),
     )(*results)
 
 

time: 49.4 us -> 45.8 us (0.927)
  Pallas kernels: 46.8 us -> 44.5 us
  local copies, waits for them, and re-layouts: 1.78 us -> 0 us
    pallas_call x2, Pallas kernels: 46.8 us -> 44.5 us  [the longest x1 43.2 us: body(): pl.pallas_call(functools.partial(kernel, nb, na, heads), out_shape=shapes...]
    unnamed x6 -> x0, local copies, waits for them, and re-layouts: 1.78 us -> none
where the time goes in v5:
time: 45.8 us; the launch traced here: 45.2 us
  Pallas kernels  44.5 us (97%)
  between operations  0.64 us (1%)
    pallas_call x1, Pallas kernels, body(): pl.pallas_call(functools.partial(kernel, nb, na, heads), out_shape=shapes...  43.2 us
    pallas_call x1, Pallas kernels, body(): pl.pallas_call(place, out_shape=shapes, in_specs=[hbm, hbm, hbm], out_spe...  1.37 us

profile of v5, /device:TPU:1, one launch (start us, length us, event | category | flops | bytes accessed | tf_op | source)
XLA Modules:
  0.0 45.2 jit_solution(8509902624457231828)
XLA Ops:
  0.6 43.2 %shard_map.76 = (f32[32,128]{1,0:T(8,128)}, f32[32,128]{1,0:T(8,128)}, f32[2,512]{1,0:T(2,128)}) custom-call(bf16[512,256]{1,0:T(8,128)(2,1)} %q_hbm.1, bf16[1024,256]{1,0:T(8,128)(2,1)} %k_hbm.1, bf16[512,128]{1,0:T(8,128)(2,1)} %c_hbm.1, bf16[1024,128]{1,0:T(8,128)(2,1)} %b_hbm.1, f32[2,512]{1,0:T(2,128)} %rate_hbm.1), custom_call_target="tpu_custom_call" | custom-call | tf_op jit(solution)/shard_map/pallas_call | solution.py:708
  43.8 1.4 %shard_map.77 = (f32[32,128]{1,0:T(8,128)}, f32[32,128]{1,0:T(8,128)}, f32[2,512]{1,0:T(2,128)}) custom-call(f32[32,128]{1,0:T(8,128)} %get-tuple-element.6.gc_in, f32[32,128]{1,0:T(8,128)} %get-tuple-element.7.gb_in, f32[2,512]{1,0:T(2,128)} %get-tuple-element.8.gr_in), custom_call_target="tpu_custom_call" | custom-call | tf_op jit(solution)/shard_map/pallas_call | solution.py:766

commit v6 on v5

--- a/solution.py
+++ b/solution.py
@@ -69,6 +69,7 @@
     krate_ref,
     rfold_ref,
     stat_ref,
+    peak_ref,
     cs_ref,
     fold_ref,
     col_ref,
@@ -291,9 +292,9 @@
             return total
 
         total = lax.fori_loop(0, steps, expo_turn, jnp.zeros((8, qn), jnp.float32))
-        stat_ref[ka, h : h + 1, :] = peak
-        stat_ref[ka, heads + h : heads + h + 1, :] = jnp.sum(
-            total, axis=0, keepdims=True
+        peak_ref[h : h + 1, :] = peak
+        stat_ref[ka, h : h + 1, :] = peak + jnp.log2(
+            jnp.sum(total, axis=0, keepdims=True)
         )
 
     def stats(first, last):
@@ -309,13 +310,7 @@
 
     @pl.when(live)
     def _():
-        stat_init = jnp.concatenate(
-            [
-                jnp.full((heads, qn), NEGATIVE, jnp.float32),
-                jnp.zeros((heads, qn), jnp.float32),
-            ],
-            axis=0,
-        )
+        stat_init = jnp.full((heads, qn), NEGATIVE, jnp.float32)
 
         @pl.loop(z + 1, na)
         def _(slot):
@@ -457,12 +452,10 @@
             def _():
                 stat_copy(slot, slot).wait_recv()
 
-        peaks = stat_ref[:, 0:heads, :]
-        totals = stat_ref[:, heads : 2 * heads, :]
-        peak = jnp.max(peaks, axis=0)
-        total = jnp.sum(totals * jnp.exp2(peaks - peak[None]), axis=0)
-        own_peak = stat_ref[ka, 0:heads, :]
-        scaling = jnp.exp2(own_peak - peak) / total
+        parts = stat_ref[...]
+        peak = jnp.max(parts, axis=0)
+        total = jnp.sum(jnp.exp2(parts - peak[None]), axis=0)
+        scaling = jnp.exp2(peak_ref[...] - (peak + jnp.log2(total)))
 
         def send_grad_b(t):
             gx_copy(t * per_chunk, per_chunk).wait_recv()
@@ -510,7 +503,11 @@
         def _(target):
             fold_copy(pb, target).start()
 
-        def weight_turn(t, carry):
+        def turn_chunk(n):
+            return lax.rem(n + z // per_chunk, steps)
+
+        def weight_turn(n, carry):
+            t = turn_chunk(n)
             out = jnp.zeros((CHUNK, cols), jnp.float32)
             for h in range(heads):
                 weights = []
@@ -526,25 +523,28 @@
                 per_chunk, 2, gb_rows, cols
             )
             gx_copy(t * per_chunk, per_chunk).start()
+
+            @pl.when(n > 0)
+            def _():
+                send_grad_b(turn_chunk(n - 1))
+
             return carry
 
         lax.fori_loop(0, steps, weight_turn, 0)
 
+        flats = []
         for h in range(heads):
             slope_ref[ka, h : h + 1, 0:qn] = jnp.sum(
                 rs_ref[h, 0], axis=0, keepdims=True
             ) - scaling[h : h + 1, :] * jnp.sum(rs_ref[h, 1], axis=0, keepdims=True)
-            flat = dot(
-                bt_ref[h * state : (h + 1) * state, :], w_ref[h], ((1,), (0,))
+            flats.append(
+                dot(bt_ref[h * state : (h + 1) * state, :], w_ref[h], ((1,), (0,)))
             )
-            gcown_ref[:, h * state : (h + 1) * state] = jnp.transpose(flat * factor)
+        send_grad_b(turn_chunk(steps - 1))
+        gcown_ref[...] = jnp.transpose(jnp.concatenate(flats, axis=0) * factor)
         gcsend_ref[...] = (
             gcown_ref[...].reshape(na, gc_rows, cols).astype(jnp.bfloat16)
         )
-
-        @pl.loop(0, steps)
-        def _(n):
-            send_grad_b(lax.rem(n + z // per_chunk, steps))
 
         @pl.loop(1, na)
         def _(k):
@@ -726,7 +726,8 @@
             pltpu.VMEM((heads, qn), f32),
             pltpu.VMEM((2, heads, qn), f32),
             pltpu.VMEM((nb, heads, 128), f32),
-            pltpu.VMEM((na, 2 * heads, qn), f32),
+            pltpu.VMEM((na, heads, qn), f32),
+            pltpu.VMEM((heads, qn), f32),
             pltpu.VMEM((kn // 128, heads, 128), f32),
             pltpu.VMEM((nb, heads, 128), f32),
             pltpu.VMEM((nb, qn // 128, heads, 128), f32),

time: 45.8 us -> 45.3 us (0.989)
  the two profiles are of different devices: /device:TPU:1 before, /device:TPU:2 now
where the time goes in v6:
time: 45.3 us; the launch traced here: 45.1 us
  Pallas kernels  44.4 us (98%)
  between operations  0.64 us (1%)
    pallas_call x1, Pallas kernels, body(): pl.pallas_call(functools.partial(kernel, nb, na, heads), out_shape=shapes...  43.1 us
    pallas_call x1, Pallas kernels, body(): pl.pallas_call(place, out_shape=shapes, in_specs=[hbm, hbm, hbm], out_spe...  1.37 us

profile of v6, /device:TPU:2, one launch (start us, length us, event | category | flops | bytes accessed | tf_op | source)
XLA Modules:
  0.0 45.1 jit_solution(16261803644520621216)
XLA Ops:
  0.6 43.1 %shard_map.76 = (f32[32,128]{1,0:T(8,128)}, f32[32,128]{1,0:T(8,128)}, f32[2,512]{1,0:T(2,128)}) custom-call(bf16[512,256]{1,0:T(8,128)(2,1)} %q_hbm.1, bf16[1024,256]{1,0:T(8,128)(2,1)} %k_hbm.1, bf16[512,128]{1,0:T(8,128)(2,1)} %c_hbm.1, bf16[1024,128]{1,0:T(8,128)(2,1)} %b_hbm.1, f32[2,512]{1,0:T(2,128)} %rate_hbm.1), custom_call_target="tpu_custom_call" | custom-call | tf_op jit(solution)/shard_map/pallas_call | solution.py:708
  43.7 1.4 %shard_map.77 = (f32[32,128]{1,0:T(8,128)}, f32[32,128]{1,0:T(8,128)}, f32[2,512]{1,0:T(2,128)}) custom-call(f32[32,128]{1,0:T(8,128)} %get-tuple-element.6.gc_in, f32[32,128]{1,0:T(8,128)} %get-tuple-element.7.gb_in, f32[2,512]{1,0:T(2,128)} %get-tuple-element.8.gr_in), custom_call_target="tpu_custom_call" | custom-call | tf_op jit(solution)/shard_map/pallas_call | solution.py:767

commit v7 on v6

--- a/solution.py
+++ b/solution.py
@@ -70,6 +70,9 @@
     rfold_ref,
     stat_ref,
     peak_ref,
+    total_ref,
+    mix_ref,
+    scale_ref,
     cs_ref,
     fold_ref,
     col_ref,
@@ -264,49 +267,43 @@
 
     scale2 = LOG2E / math.sqrt(dh)
 
-    def head_stats(h, masked):
-        lanes = slice(h * dh, (h + 1) * dh)
-
-        def score_turn(t, peak):
-            s = dot(k_ref[chunk_rows(t), lanes], q_ref[:, lanes], ((1,), (1,)))
-            for n in range(pieces):
-                part = s[n * PIECE : (n + 1) * PIECE] * scale2
-                if masked:
-                    part = jnp.where(mask_of(t, n), part, NEGATIVE)
-                s_ref[h, piece_rows(t, n), :] = part
-                for k in range(0, PIECE, 8):
-                    peak = jnp.maximum(peak, part[k : k + 8])
-            return peak
-
-        peak = lax.fori_loop(
-            0, steps, score_turn, jnp.full((8, qn), NEGATIVE, jnp.float32)
-        )
-        peak = jnp.max(peak, axis=0, keepdims=True)
-
-        def expo_turn(t, total):
-            for n in range(pieces):
-                e = jnp.exp2(s_ref[h, piece_rows(t, n), :] - peak)
-                s_ref[h, piece_rows(t, n), :] = e
-                for k in range(0, PIECE, 8):
-                    total = total + e[k : k + 8]
-            return total
-
-        total = lax.fori_loop(0, steps, expo_turn, jnp.zeros((8, qn), jnp.float32))
-        peak_ref[h : h + 1, :] = peak
-        stat_ref[ka, h : h + 1, :] = peak + jnp.log2(
-            jnp.sum(total, axis=0, keepdims=True)
-        )
-
-    def stats(first, last):
-        @pl.when(diagonal)
-        def _():
-            for h in range(first, last):
-                head_stats(h, True)
-
-        @pl.when(z > ka)
-        def _():
-            for h in range(first, last):
-                head_stats(h, False)
+    def stats(masked):
+        def score_turn(t, carry):
+            rows = chunk_rows(t)
+            every = [
+                dot(
+                    k_ref[rows, h * dh : (h + 1) * dh],
+                    q_ref[:, h * dh : (h + 1) * dh],
+                    ((1,), (1,)),
+                )
+                for h in range(heads)
+            ]
+            for h in range(heads):
+                parts = []
+                peak = jnp.full((8, qn), NEGATIVE, jnp.float32)
+                for n in range(pieces):
+                    part = every[h][n * PIECE : (n + 1) * PIECE]
+                    if masked:
+                        part = jnp.where(mask_of(t, n), part, NEGATIVE)
+                    parts.append(part)
+                    for k in range(0, PIECE, 8):
+                        peak = jnp.maximum(peak, part[k : k + 8])
+                peak = jnp.max(peak, axis=0, keepdims=True)
+                total = jnp.zeros((8, qn), jnp.float32)
+                for n in range(pieces):
+                    e = jnp.exp2((parts[n] - peak) * scale2)
+                    s_ref[h, piece_rows(t, n), :] = e
+                    for k in range(0, PIECE, 8):
+                        total = total + e[k : k + 8]
+                peak_ref[t, h : h + 1, :] = peak * scale2
+                total_ref[t, h : h + 1, :] = jnp.sum(total, axis=0, keepdims=True)
+            return carry
+
+        lax.fori_loop(0, steps, score_turn, 0)
+        peaks = peak_ref[...]
+        peak = jnp.max(peaks, axis=0)
+        total = jnp.sum(total_ref[...] * jnp.exp2(peaks - peak[None]), axis=0)
+        stat_ref[ka] = peak + jnp.log2(total)
 
     @pl.when(live)
     def _():
@@ -319,7 +316,13 @@
     loads[0].wait()
     loads[1].wait()
 
-    stats(0, heads)
+    @pl.when(diagonal)
+    def _():
+        stats(True)
+
+    @pl.when(z > ka)
+    def _():
+        stats(False)
 
     for load in loads[2:]:
         load.wait()
@@ -408,7 +411,8 @@
                 inners = [dot(b_rows, ch_ref[h], ((1,), (1,))) for h in range(heads)]
                 new_sums = []
                 for h in range(heads):
-                    squares, mixed = sums[h]
+                    squares = sums[h]
+                    mixed = jnp.zeros((8, qn), jnp.float32)
                     for m in range(pieces):
                         at = piece_rows(t, m)
                         column = kcol_ref[h, at, :]
@@ -427,16 +431,16 @@
                         for k in range(0, PIECE, 8):
                             squares = squares + square[k : k + 8]
                             mixed = mixed + mix[k : k + 8]
-                    new_sums.append((squares, mixed))
+                    new_sums.append(squares)
+                    mix_ref[t, h : h + 1, :] = jnp.sum(mixed, axis=0, keepdims=True)
                 return tuple(new_sums)
 
             zero = jnp.zeros((8, qn), jnp.float32)
             sums = lax.fori_loop(
-                0, steps, student_turn, tuple((zero, zero) for _ in range(heads))
+                0, steps, student_turn, tuple(zero for _ in range(heads))
             )
             for h in range(heads):
-                rs_ref[h, 0] = sums[h][0]
-                rs_ref[h, 1] = sums[h][1]
+                rs_ref[h] = sums[h]
 
         @pl.when(diagonal)
         def _():
@@ -455,7 +459,7 @@
         parts = stat_ref[...]
         peak = jnp.max(parts, axis=0)
         total = jnp.sum(jnp.exp2(parts - peak[None]), axis=0)
-        scaling = jnp.exp2(peak_ref[...] - (peak + jnp.log2(total)))
+        scale_ref[...] = jnp.exp2(peak_ref[...] - (peak + jnp.log2(total))[None])
 
         def send_grad_b(t):
             gx_copy(t * per_chunk, per_chunk).wait_recv()
@@ -477,10 +481,11 @@
         def column_turn(t, carry):
             for h in range(heads):
                 folds = []
+                scaling = scale_ref[t, h : h + 1, :]
                 for m in range(pieces):
                     at = piece_rows(t, m)
                     student = st_ref[h, at, :]
-                    grad = student - s_ref[h, at, :] * scaling[h : h + 1, :]
+                    grad = student - s_ref[h, at, :] * scaling
                     folds.append(fold_lanes(grad * student))
                 fold = jnp.concatenate(folds, axis=0)
                 for k in range(blocks):
@@ -503,18 +508,15 @@
         def _(target):
             fold_copy(pb, target).start()
 
-        def turn_chunk(n):
-            return lax.rem(n + z // per_chunk, steps)
-
-        def weight_turn(n, carry):
-            t = turn_chunk(n)
+        def weight_turn(t, carry):
             out = jnp.zeros((CHUNK, cols), jnp.float32)
             for h in range(heads):
                 weights = []
+                scaling = scale_ref[t, h : h + 1, :]
                 for m in range(pieces):
                     at = piece_rows(t, m)
                     student = st_ref[h, at, :]
-                    grad = student - s_ref[h, at, :] * scaling[h : h + 1, :]
+                    grad = student - s_ref[h, at, :] * scaling
                     weights.append((grad * dec_ref[h, at, :]).astype(jnp.bfloat16))
                 weight = jnp.concatenate(weights, axis=0)
                 w_ref[h, chunk_rows(t), :] = weight
@@ -524,9 +526,9 @@
             )
             gx_copy(t * per_chunk, per_chunk).start()
 
-            @pl.when(n > 0)
-            def _():
-                send_grad_b(turn_chunk(n - 1))
+            @pl.when(t > 0)
+            def _():
+                send_grad_b(t - 1)
 
             return carry
 
@@ -534,13 +536,14 @@
 
         flats = []
         for h in range(heads):
-            slope_ref[ka, h : h + 1, 0:qn] = jnp.sum(
-                rs_ref[h, 0], axis=0, keepdims=True
-            ) - scaling[h : h + 1, :] * jnp.sum(rs_ref[h, 1], axis=0, keepdims=True)
+            slope_ref[ka, h : h + 1, 0:qn] = jnp.sum(rs_ref[h], axis=0, keepdims=True)
             flats.append(
                 dot(bt_ref[h * state : (h + 1) * state, :], w_ref[h], ((1,), (0,)))
             )
-        send_grad_b(turn_chunk(steps - 1))
+        slope_ref[ka, :, 0:qn] = slope_ref[ka, :, 0:qn] - jnp.sum(
+            scale_ref[...] * mix_ref[...], axis=0
+        )
+        send_grad_b(steps - 1)
         gcown_ref[...] = jnp.transpose(jnp.concatenate(flats, axis=0) * factor)
         gcsend_ref[...] = (
             gcown_ref[...].reshape(na, gc_rows, cols).astype(jnp.bfloat16)
@@ -600,50 +603,6 @@
     sums = lax.fori_loop(0, jnp.minimum(ka, z + 1), gc_turn, gc_ref[...])
     gc_ref[...] = lax.fori_loop(ka + 1, z + 1, gc_turn, sums)
 
-    def gb_turn(slot, total):
-        gb_copy(slot, slot).wait_recv()
-        return total + gbrecv_ref[slot].astype(jnp.float32)
-
-    sums = lax.fori_loop(ka, z, gb_turn, gb_ref[...])
-    gb_ref[...] = lax.fori_loop(jnp.maximum(ka, z + 1), nz, gb_turn, sums)
-
-    @pl.when(live)
-    def _():
-        to(
-            gbpart_ref.at[pl.ds(0, nz), other], gbsib_ref, gx_send, gx_recv.at[0], (sibling, ka)
-        ).wait_send()
-
-        for part in range(2):
-
-            @pl.when(pb != first + part)
-            def _(part=part):
-                col_copy(part, pb).wait_send()
-
-        @pl.loop(pb + 1, nb)
-        def _(target):
-            @pl.when(diagonal)
-            def _():
-                krate_copy(core, target).wait_send()
-
-            @pl.when(jnp.logical_not(diagonal))
-            def _():
-                rfold_copy(pb, target).wait_send()
-
-        @pl.loop(first, pb)
-        def _(target):
-            fold_copy(pb, target).wait_send()
-
-        @pl.loop(0, z + 1)
-        def _(target):
-            @pl.when(target != ka)
-            def _():
-                stat_copy(ka, target).wait_send()
-
-        rest = pl.ds(0, na - 1)
-        to(gcsend_ref.at[rest], gcrecv_ref.at[rest], gc_send, gc_recv.at[0], (pb, ka)).wait_send()
-        rest = pl.ds(0, nz - 1)
-        to(gbsend_ref.at[rest], gbrecv_ref.at[rest], gb_send, gb_recv.at[0], (pb, ka)).wait_send()
-
     def slope_turn(slot, total):
         slope_copy(slot, slot).wait_recv()
         return total + slope_ref[slot]
@@ -660,6 +619,50 @@
     scan_ref[0:heads, :] = slope
     suffix = jnp.sum(slope, axis=1, keepdims=True) - lane_prefix(scan_ref[...])[0:heads, :]
     gr_ref[...] = -factor * (suffix + slope + after)
+
+    @pl.when(live)
+    def _():
+        to(
+            gbpart_ref.at[pl.ds(0, nz), other], gbsib_ref, gx_send, gx_recv.at[0], (sibling, ka)
+        ).wait_send()
+
+        for part in range(2):
+
+            @pl.when(pb != first + part)
+            def _(part=part):
+                col_copy(part, pb).wait_send()
+
+        @pl.loop(pb + 1, nb)
+        def _(target):
+            @pl.when(diagonal)
+            def _():
+                krate_copy(core, target).wait_send()
+
+            @pl.when(jnp.logical_not(diagonal))
+            def _():
+                rfold_copy(pb, target).wait_send()
+
+        @pl.loop(first, pb)
+        def _(target):
+            fold_copy(pb, target).wait_send()
+
+        @pl.loop(0, z + 1)
+        def _(target):
+            @pl.when(target != ka)
+            def _():
+                stat_copy(ka, target).wait_send()
+
+        rest = pl.ds(0, na - 1)
+        to(gcsend_ref.at[rest], gcrecv_ref.at[rest], gc_send, gc_recv.at[0], (pb, ka)).wait_send()
+        rest = pl.ds(0, nz - 1)
+        to(gbsend_ref.at[rest], gbrecv_ref.at[rest], gb_send, gb_recv.at[0], (pb, ka)).wait_send()
+
+    def gb_turn(slot, total):
+        gb_copy(slot, slot).wait_recv()
+        return total + gbrecv_ref[slot].astype(jnp.float32)
+
+    sums = lax.fori_loop(ka, z, gb_turn, gb_ref[...])
+    gb_ref[...] = lax.fori_loop(jnp.maximum(ka, z + 1), nz, gb_turn, sums)
 
     @pl.when(live)
     def _():
@@ -727,12 +730,15 @@
             pltpu.VMEM((2, heads, qn), f32),
             pltpu.VMEM((nb, heads, 128), f32),
             pltpu.VMEM((na, heads, qn), f32),
-            pltpu.VMEM((heads, qn), f32),
+            pltpu.VMEM((steps, heads, qn), f32),
+            pltpu.VMEM((steps, heads, qn), f32),
+            pltpu.VMEM((steps, heads, qn), f32),
+            pltpu.VMEM((steps, heads, qn), f32),
             pltpu.VMEM((kn // 128, heads, 128), f32),
             pltpu.VMEM((nb, heads, 128), f32),
             pltpu.VMEM((nb, qn // 128, heads, 128), f32),
             pltpu.VMEM((na, heads, qn + 128), f32),
-            pltpu.VMEM((heads, 2, 8, qn), f32),
+            pltpu.VMEM((heads, 8, qn), f32),
             pltpu.VMEM((nz, 2, kn // nb, cols), f32),
             pltpu.VMEM((nz, kn // nb, cols), f32),
             pltpu.VMEM((kn // nb, cols), f32),

time: 45.3 us -> 43.4 us (0.958)
  the two profiles are of different devices: /device:TPU:2 before, /device:TPU:64 now
where the time goes in v7:
time: 43.4 us; the launch traced here: 43.2 us
  Pallas kernels  42.5 us (98%)
  between operations  0.64 us (1%)
    pallas_call x1, Pallas kernels, body(): pl.pallas_call(functools.partial(kernel, nb, na, heads), out_shape=shapes...  41.2 us
    pallas_call x1, Pallas kernels, body(): pl.pallas_call(place, out_shape=shapes, in_specs=[hbm, hbm, hbm], out_spe...  1.37 us

profile of v7, /device:TPU:64, one launch (start us, length us, event | category | flops | bytes accessed | tf_op | source)
XLA Modules:
  0.0 43.2 jit_solution(10663523753284626283)
XLA Ops:
  0.6 41.2 %shard_map.76 = (f32[32,128]{1,0:T(8,128)}, f32[32,128]{1,0:T(8,128)}, f32[2,512]{1,0:T(2,128)}) custom-call(bf16[512,256]{1,0:T(8,128)(2,1)} %q_hbm.1, bf16[1024,256]{1,0:T(8,128)(2,1)} %k_hbm.1, bf16[512,128]{1,0:T(8,128)(2,1)} %c_hbm.1, bf16[1024,128]{1,0:T(8,128)(2,1)} %b_hbm.1, f32[2,512]{1,0:T(2,128)} %rate_hbm.1), custom_call_target="tpu_custom_call" | custom-call | tf_op jit(solution)/shard_map/pallas_call | solution.py:711
  41.8 1.4 %shard_map.77 = (f32[32,128]{1,0:T(8,128)}, f32[32,128]{1,0:T(8,128)}, f32[2,512]{1,0:T(2,128)}) custom-call(f32[32,128]{1,0:T(8,128)} %get-tuple-element.6.gc_in, f32[32,128]{1,0:T(8,128)} %get-tuple-element.7.gb_in, f32[2,512]{1,0:T(2,128)} %get-tuple-element.8.gr_in), custom_call_target="tpu_custom_call" | custom-call | tf_op jit(solution)/shard_map/pallas_call | solution.py:773
